TPU v7x, 32 devices: a whole 2x2x4 slice. The times are simulated.
32 devices in a mesh: grp: 2 (over y), lon: 4 (over z), ch: 4 (over x, core).
Axes of the slice: x: 2, y: 2, z: 4, core: 2. Of those that a mesh axis runs over, the one named last changes fastest.
Arguments:
- field_in: bfloat16 [512, 64, 128], P('ch', ('grp', 'lon')), parts along dimension 1
- sea_mask: int32 [32, 128], P('lon'), may hold values 0 or 1
- fold_partner: int32 [4], replicated, may hold values from 0 to 3, as said below
- kernel: float32 [512, 7, 7], P('ch'), may hold values from -0.875 to 0.875
- ln_gain: float32 [512], replicated, may hold values from 0.5 to 1.5
- ln_shift: float32 [512], replicated, may hold values from -3 to 3
- w_in: bfloat16 [512, 1024], P(None, 'ch'), may hold values from -0.25 to 0.25
- w_out: bfloat16 [1024, 512], P('ch'), may hold values from -0.1875 to 0.1875
- layer_scale: float32 [512], P('ch'), may hold values from 0.25 to 1.75
- grad_out: bfloat16 [512, 64, 128], P('ch', ('grp', 'lon')), parts along dimension 1, may hold values from -6 to 6
Outputs:
- block_out: bfloat16 [512, 64, 128], P('ch', ('grp', 'lon')), parts along dimension 1
- grad_x: bfloat16 [512, 64, 128], P('ch', ('grp', 'lon')), parts along dimension 1
- grad_kernel: float32 [1024, 7, 7], P(('grp', 'ch')), parts along dimension 0
- grad_w_in: float32 [1024, 1024], P('grp', 'ch'), parts along dimension 0
- grad_w_out: float32 [2048, 512], P(('grp', 'ch')), parts along dimension 0
There are 2 independent parts, one for each index of `grp`. A program takes and returns all parts, laid end to end along the dimension named above; an argument that names none is the same for every part. Nothing has to cross between parts.
Inputs may be any that keep to these rules, and one draw needn't show every extreme that they name: fold_partner[fold_partner[t]] = t for every tile t; a tile may face itself, and at least one tile faces another tile.
All inputs are finite; a program needn't handle non-finite values. No bound on the sum of `sea_mask` on one device may be relied on, other than what follows from the above.
Results may differ from a plain program's by a relative error of at most 0.0063.
Values may be sent and summed in bfloat16 or wider, within the bound.
A program may use at most 64 MiB of HBM per device.

v0:
```python
import math

import jax
import jax.numpy as jnp
from jax import lax
from jax.sharding import PartitionSpec as P

EPSILON = 1e-06


def extended_2(shard, sides, width):
    for axis, dim in sides:
        peers, length = (lax.axis_size(axis), shard.shape[dim])
        up = [(i, (i + 1) % peers) for i in range(peers)]
        down = [(j, i) for i, j in up]
        last = lax.slice_in_dim(shard, length - width, length, axis=dim)
        first = lax.slice_in_dim(shard, 0, width, axis=dim)
        before = lax.ppermute(last, axis, up)
        after = lax.ppermute(first, axis, down)
        shard = jnp.concatenate([before, shard, after], axis=dim)
    return shard


def shifted(value, axis, steps):
    count = lax.axis_size(axis)
    pairs = [(source, (source + steps) % count) for source in range(count)]
    return lax.ppermute(value, axis, pairs)


def gelu_parts(hidden):
    normal_cdf = 0.5 * (1.0 + jax.scipy.special.erf(hidden * (1.0 / math.sqrt(2.0))))
    density = jnp.exp(-0.5 * hidden * hidden) * (1.0 / math.sqrt(2.0 * math.pi))
    return (hidden * normal_cdf, normal_cdf + hidden * density)


def fold_of(rows_all, fold_partner, tile_pick, lon_dev):
    start_col = fold_partner[tile_pick] * lon_dev
    return lax.dynamic_slice_in_dim(rows_all, start_col, lon_dev, 1)[:, ::-1, :]


def body(
    field_in, sea_mask, fold_partner, kernel, ln_gain, ln_shift, w_in, w_out, layer_scale, grad_out
):
    chan_count, lon_dev, lat_count = field_in.shape
    chan_width = ln_gain.shape[0]
    tile_count = lax.axis_size("lon")
    tile_index = lax.axis_index("lon")
    chan_rank = lax.axis_index("ch")
    cell_count = lon_dev * lat_count
    ocean_f = sea_mask.astype(jnp.float32)[None]
    masked = field_in * sea_mask.astype(jnp.bfloat16)[None]
    south_rows = jnp.zeros((chan_count, lon_dev, 3), jnp.bfloat16)
    top_rows = masked[:, :, lat_count - 3 :][:, :, ::-1]
    top_all = lax.all_gather(top_rows, "lon", axis=1, tiled=True)
    tall_field = jnp.concatenate(
        [south_rows, masked, fold_of(top_all, fold_partner, tile_index, lon_dev)], axis=2
    )
    extended = extended_2(tall_field, (("lon", 1),), 3)
    extended_f = extended.astype(jnp.float32)
    mix_field = jnp.zeros((chan_count, lon_dev, lat_count), jnp.float32)
    for row_tap in range(7):
        for col_tap in range(7):
            mix_field = (
                mix_field
                + kernel[:, row_tap, col_tap][:, None, None]
                * extended_f[:, row_tap : row_tap + lon_dev, col_tap : col_tap + lat_count]
            )
    grad_f = grad_out.astype(jnp.float32)
    scaled_grad = (
        (ocean_f * layer_scale[:, None, None] * grad_f)
        .astype(jnp.bfloat16)
        .reshape(chan_count, cell_count)
    )
    offset = chan_rank * chan_count
    gain_own = lax.dynamic_slice_in_dim(ln_gain, offset, chan_count)
    shift_own = lax.dynamic_slice_in_dim(ln_shift, offset, chan_count)
    sum_one, sum_two = lax.psum(
        (jnp.sum(mix_field, axis=0), jnp.sum(mix_field * mix_field, axis=0)), "ch"
    )
    mean_cell = sum_one / chan_width
    inv_sigma = lax.rsqrt(sum_two / chan_width - mean_cell * mean_cell + EPSILON)
    centred = (mix_field - mean_cell) * inv_sigma
    normed = (
        (centred * gain_own[:, None, None] + shift_own[:, None, None])
        .astype(jnp.bfloat16)
        .reshape(chan_count, cell_count)
    )
    normed_all = lax.all_gather(normed, "ch", axis=0, tiled=True)
    hidden = lax.dot_general(
        normed_all, w_in, (((0,), (0,)), ((), ())), preferred_element_type=jnp.float32
    )
    activation, gelu_slope = gelu_parts(hidden)
    activated = activation.astype(jnp.bfloat16)
    w_rows = w_out
    branch = lax.psum_scatter(
        lax.dot_general(
            w_rows, activated, (((0,), (1,)), ((), ())), preferred_element_type=jnp.float32
        ),
        "ch",
        scatter_dimension=0,
        tiled=True,
    )
    grads_all = lax.all_gather(scaled_grad, "ch", axis=0, tiled=True)
    activated_grad = lax.dot_general(
        grads_all, w_out, (((0,), (1,)), ((), ())), preferred_element_type=jnp.float32
    )
    gw_out = lax.dot_general(
        activated, grads_all, (((0,), (1,)), ((), ())), preferred_element_type=jnp.float32
    )
    hidden_grad = (activated_grad * gelu_slope).astype(jnp.bfloat16)
    gw_in = lax.dot_general(
        normed_all, hidden_grad, (((1,), (0,)), ((), ())), preferred_element_type=jnp.float32
    )
    w_rows = w_in
    normed_grad = lax.psum_scatter(
        lax.dot_general(
            w_rows, hidden_grad, (((1,), (1,)), ((), ())), preferred_element_type=jnp.float32
        ),
        "ch",
        scatter_dimension=0,
        tiled=True,
    ).reshape(chan_count, lon_dev, lat_count)
    scaled_normed = normed_grad * gain_own[:, None, None]
    grad_one, grad_two = lax.psum(
        (jnp.sum(scaled_normed, axis=0), jnp.sum(scaled_normed * centred, axis=0)), "ch"
    )
    mixed_grad = inv_sigma * (
        scaled_normed - grad_one / chan_width - centred * (grad_two / chan_width)
    )
    block_out = (
        ocean_f
        * (
            field_in.astype(jnp.float32)
            + layer_scale[:, None, None] * branch.reshape(chan_count, lon_dev, lat_count)
        )
    ).astype(jnp.bfloat16)
    tap_sums = []
    for row_tap in range(7):
        for col_tap in range(7):
            tap_sums.append(
                jnp.sum(
                    extended_f[:, row_tap : row_tap + lon_dev, col_tap : col_tap + lat_count]
                    * mixed_grad,
                    axis=(1, 2),
                )
            )
    kernel_grad = jnp.stack(tap_sums, axis=1).reshape(chan_count, 7, 7)
    padded = jnp.pad(mixed_grad, ((0, 0), (6, 6), (6, 6)))
    spread = jnp.zeros((chan_count, lon_dev + 6, lat_count + 6), jnp.float32)
    for row_tap in range(7):
        for col_tap in range(7):
            spread = (
                spread
                + kernel[:, row_tap, col_tap][:, None, None]
                * padded[
                    :,
                    6 - row_tap : 6 - row_tap + lon_dev + 6,
                    6 - col_tap : 6 - col_tap + lat_count + 6,
                ]
            )
    from_east = shifted(spread[:, :3], "lon", -1)
    from_west = shifted(spread[:, lon_dev + 3 :], "lon", 1)
    tall_grad = spread[:, 3 : 3 + lon_dev]
    tall_grad = tall_grad.at[:, :3].add(from_west)
    tall_grad = tall_grad.at[:, lon_dev - 3 :].add(from_east)
    fold_grad = tall_grad[:, :, 3 + lat_count :]
    fold_all = lax.all_gather(fold_grad, "lon", axis=1, tiled=True)
    fold_back = fold_of(fold_all, fold_partner, tile_index, lon_dev)[:, :, ::-1]
    field_grad = tall_grad[:, :, 3 : 3 + lat_count].at[:, :, lat_count - 3 :].add(fold_back)
    grad_x = (ocean_f * (grad_f + field_grad)).astype(jnp.bfloat16)
    factor = 1.0 / math.sqrt(tile_count * lon_dev * lat_count)
    kernel_total, w_in_total, w_out_total = lax.psum((kernel_grad, gw_in, gw_out), "lon")
    return (block_out, grad_x, kernel_total * factor, w_in_total * factor, w_out_total * factor)


def solution(mesh):
    placed = (
        P("ch", ("grp", "lon"), None),
        P("lon", None),
        P(),
        P("ch", None, None),
        P(),
        P(),
        P(None, "ch"),
        P("ch", None),
        P("ch"),
        P("ch", ("grp", "lon"), None),
    )
    return jax.shard_map(
        body,
        mesh=mesh,
        in_specs=placed,
        out_specs=(
            P("ch", ("grp", "lon"), None),
            P("ch", ("grp", "lon"), None),
            P(("grp", "ch"), None, None),
            P("grp", "ch"),
            P(("grp", "ch"), None),
        ),
        check_vma=False,
    )
```

profile of v0, /device:TPU:0, one launch (start us, length us, event | category | flops | bytes accessed | tf_op | source)
XLA Modules:
  0.0 277.7 jit_solution(15667772636311070049)
XLA Ops:
  7.2 1.2 dynamic_slice.16
  9.1 0.8 fusion.110
  10.0 1.2 copy.24
  11.2 0.2 broadcast_multiply_fusion.2
  11.5 13.6 %all_gather.12 = bf16[128,32,3]{0,1,2:T(8,128)(2,1)S(1)} all-gather(bf16[128,8,3]{0,1,2:T(8,128)(2,1)S(1)} %rev.10), channel_id=1, replica_groups=mesh['grp'=2,'lon'=4,'ch'=4] {'lon'}, dimensions={1}, use_global_device_ids=true | all-gather | bytes 30720 | tf_op jit(solution)/shard_map/all_gather | solution.py:54
  25.1 0.2 pad_maximum_fusion
  25.4 1.6 collective-permute-start
  27.0 2.3 collective-permute-start.1
  29.4 0.8 dynamic_slice.18
  30.1 0.8 dynamic_slice.19
  30.9 1.6 collective-permute-done
  32.5 1.1 collective-permute-done.1
  33.6 4.0 %fusion.107 = (f32[8,128]{1,0:T(8,128)S(1)}, f32[8,128]{1,0:T(8,128)S(1)}, f32[128,8,128]{0,2,1:T(8,128)S(1)}) fusion(f32[128,14,134]{0,2,1:T(8,128)S(1)} %maximum_convert_fusion, f32[128]{0:T(128)S(1)} %get-tuple-element.161, f32[128]{0:T(128)S(1)} %get-tuple-element.162, f32[128]{0:T(128)S(1)} %get-tuple-element.115, f32[128]{0:T(128)S(1)} %get-tuple-element.116, ...), kind=kLoop, calls=%fused_computation.285 | loop fusion | flops 13105152 | bytes 26247680 | tf_op jit(solution)/shard_map/reduce_sum | solution.py:78
  37.6 5.9 %all-reduce.2 = (f32[8,128]{1,0:T(8,128)S(1)}, f32[8,128]{1,0:T(8,128)S(1)}) all-reduce(f32[8,128]{1,0:T(8,128)S(1)} %get-tuple-element.101, f32[8,128]{1,0:T(8,128)S(1)} %get-tuple-element.100), channel_id=1, replica_groups=mesh['grp'=2,'lon'=4,'ch'=4] {'ch'}, use_global_device_ids=true, to_apply=%region_3.0 | all-reduce | flops 2048 | bytes 16384 | tf_op jit(solution)/shard_map/psum | solution.py:77
  43.5 1.0 add_convert_fusion
  44.7 17.4 %all-gather.3.cloned.1.call-done = bf16[512,1024]{0,1:T(8,128)(2,1)} async-done(((bf16[128,1024]{0,1:T(8,128)(2,1)}), bf16[512,1024]{0,1:T(8,128)(2,1)}) %all-gather.3.cloned.1.call-update) | async-done | bytes 1048592 | tf_op jit(solution)/shard_map/all_gather | solution.py:88
  62.1 2.6 multiply_convert_fusion
  64.8 1.8 convolution_bitcast_fusion.1
  66.6 0.2 copy.22
  66.9 0.2 copy.28
  67.1 31.0 %reduce-scatter.3.cloned.1.call-done = f32[128,1024]{0,1:T(8,128)} async-done(((f32[512,1024]{0,1:T(8,128)}), f32[128,1024]{0,1:T(8,128)}) %reduce-scatter.3.cloned.1.call-update) | async-done | bytes 524304 | tf_op jit(solution)/shard_map/reduce_scatter | solution.py:95
  98.1 2.0 fusion.102
  100.2 17.0 %all-gather.5.cloned.1.call-done = bf16[512,1024]{0,1:T(8,128)(2,1)} async-done(((bf16[128,1024]{0,1:T(8,128)(2,1)}), bf16[512,1024]{0,1:T(8,128)(2,1)}) %all-gather.5.cloned.1.call-update) | async-done | bytes 1048592 | tf_op jit(solution)/shard_map/all_gather | solution.py:103
  117.2 2.6 fusion.112
  119.9 0.6 fusion
  120.5 0.6 copy-done.3
  121.1 1.3 fusion.111
  122.4 1.8 convolution_bitcast_fusion
  124.3 0.9 copy.31
  125.2 49.6 %all-reduce.6.cloned.1.call-done = (f32[512,256]{1,0:T(8,128)}, f32[256,512]{1,0:T(8,128)}) async-done(((f32[512,256]{1,0:T(8,128)}, f32[256,512]{1,0:T(8,128)}), (f32[512,256]{1,0:T(8,128)}, f32[256,512]{1,0:T(8,128)})) %all-reduce.6.cloned.1.call-update) | async-done | bytes 1048592 | tf_op jit(solution)/shard_map/psum | solution.py:172
  174.7 1.9 broadcast_multiply_fusion
  176.6 1.9 broadcast_multiply_fusion.1
  178.5 29.4 %reduce-scatter.5.cloned.1.call-done = f32[128,1024]{0,1:T(8,128)} async-done(((f32[512,1024]{0,1:T(8,128)}), f32[128,1024]{0,1:T(8,128)}) %reduce-scatter.5.cloned.1.call-update) | async-done | bytes 524304 | tf_op jit(solution)/shard_map/reduce_scatter | solution.py:115
  207.9 1.5 multiply_reduce_fusion.49
  209.5 1.3 multiply_reduce_fusion.50
  210.7 6.0 %all-reduce.1 = (f32[8,128]{1,0:T(8,128)S(1)}, f32[8,128]{1,0:T(8,128)S(1)}) all-reduce(f32[8,128]{1,0:T(8,128)S(1)} %multiply_reduce_fusion.49, f32[8,128]{1,0:T(8,128)S(1)} %bitcast.177), channel_id=1, replica_groups=mesh['grp'=2,'lon'=4,'ch'=4] {'ch'}, use_global_device_ids=true, to_apply=%region_9.0 | all-reduce | flops 2048 | bytes 16384 | tf_op jit(solution)/shard_map/psum | solution.py:124
  216.8 2.5 multiply_reduce_fusion
  219.3 0.9 multiply_reduce_fusion.18
  220.2 0.7 multiply_reduce_fusion.36
  220.9 8.0 %fusion.98 = f32[128,14,134]{0,2,1:T(8,128)S(1)} fusion(f32[128,8,128]{0,2,1:T(8,128)S(1)} %get-tuple-element.108, f32[128]{0:T(128)S(1)} %get-tuple-element.161, f32[128]{0:T(128)S(1)} %get-tuple-element.162, f32[128]{0:T(128)S(1)} %get-tuple-element.115, f32[128]{0:T(128)S(1)} %get-tuple-element.116, f32[128]{0:T(128)S(1)} %get-tuple-element.117, ...), kind=kLoop, calls=%fused_computation.153 | loop fusion | flops 23292416 | bytes 1509888 | tf_op jit(solution)/shard_map/add | solution.py:153
  229.1 19.3 %psum.53 = f32[128,7,7]{0,2,1:T(8,128)S(1)} all-reduce(f32[128,7,7]{0,2,1:T(8,128)S(1)} %reshape.129), channel_id=1, replica_groups=mesh['grp'=2,'lon'=4,'ch'=4] {'lon'}, use_global_device_ids=true, to_apply=%region_59.60 | all-reduce | flops 6272 | bytes 50176 | tf_op jit(solution)/shard_map/psum | solution.py:172
  248.5 3.8 %collective-permute-start.3 = (f32[128,3,134]{0,2,1:T(8,128)S(1)}, f32[128,3,134]{0,2,1:T(8,128)S(1)}, u32[]{:S(2)}, u32[]{:S(2)}) collective-permute-start(f32[128,3,134]{0,2,1:T(8,128)S(1)} %get-tuple-element.110), channel_id=1, source_target_pairs={{0,12},{4,0},{8,4},{12,8},{1,13},{5,1},{9,5},{13,9},{2,14},{6,2},{... | collective-permute-start | bytes 617480 | tf_op jit(solution)/shard_map/ppermute | solution.py:27
  252.3 0.6 broadcast_multiply_fusion.3
  252.9 3.3 %collective-permute-done.2 = f32[128,3,134]{0,2,1:T(8,128)S(1)} collective-permute-done((f32[128,3,134]{0,2,1:T(8,128)S(1)}, f32[128,3,134]{0,2,1:T(8,128)S(1)}, u32[]{:S(2)}, u32[]{:S(2)}) %collective-permute-start.2) | collective-permute-done | bytes 205856 | tf_op jit(solution)/shard_map/ppermute | solution.py:27
  256.2 0.4 collective-permute-done.3
  256.8 13.1 %all_gather.15 = f32[128,32,3]{0,1,2:T(8,128)S(1)} all-gather(f32[128,8,3]{0,1,2:T(8,128)S(1)} %copy.29), channel_id=1, replica_groups=mesh['grp'=2,'lon'=4,'ch'=4] {'lon'}, dimensions={1}, use_global_device_ids=true | all-gather | bytes 61440 | tf_op jit(solution)/shard_map/all_gather | solution.py:167
  270.1 0.2 fusion.104
  270.3 0.9 copy.32
  (59 shorter events, 1.4 us)
Async XLA Ops:
  7.2 54.9 %copy-start = (bf16[512,256]{1,0:T(8,128)(2,1)S(1)}, bf16[512,256]{1,0:T(8,128)(2,1)}, u32[]{:S(2)}) copy-start(bf16[512,256]{1,0:T(8,128)(2,1)} %param.22) | copy-start | bytes 786436
  7.2 22.1 %copy-start.7 = (f32[128,7,7]{0,2,1:T(8,128)S(1)}, f32[128,7,7]{0,2,1:T(8,128)}, u32[]{:S(2)}) copy-start(f32[128,7,7]{0,2,1:T(8,128)} %param.19) | copy-start | bytes 75268
  7.2 54.9 %all-gather.3.cloned.1.call-start = ((), (), s32[]{:S(2)}) async-start(), calls=%async_computation.2 | async-start | bytes 1310720 | tf_op jit(solution)/shard_map/all_gather | solution.py:88
  25.4 7.0 %collective-permute-start = (bf16[128,3,134]{0,1,2:T(4,128)(2,1)S(1)}, bf16[128,3,134]{0,1,2:T(4,128)(2,1)S(1)}, u32[]{:S(2)}, u32[]{:S(2)}) collective-permute-start(bf16[128,3,134]{0,1,2:T(4,128)(2,1)S(1)} %get-tuple-element.112), channel_id=1, source_target_pairs={{0,4},{4,8},{8,12},{12,0},{1,5},{5,9},{9,13},{13,1},{2,6},{6,10},{... | collective-permute-start | bytes 308744 | tf_op jit(solution)/shard_map/ppermute | solution.py:18
  27.0 6.5 %collective-permute-start.1 = (bf16[128,3,134]{0,1,2:T(4,128)(2,1)S(1)}, bf16[128,3,134]{0,1,2:T(4,128)(2,1)S(1)}, u32[]{:S(2)}, u32[]{:S(2)}) collective-permute-start(bf16[128,3,134]{0,1,2:T(4,128)(2,1)S(1)} %get-tuple-element.113), channel_id=1, source_target_pairs={{4,0},{8,4},{12,8},{0,12},{5,1},{9,5},{13,9},{1,13},{6,2},{10,6},{... | collective-permute-start | bytes 308744 | tf_op jit(solution)/shard_map/ppermute | solution.py:19
  37.6 27.1 %copy-start.6 = (bf16[256,512]{1,0:T(8,128)(2,1)S(1)}, bf16[256,512]{1,0:T(8,128)(2,1)}, u32[]{:S(2)}) copy-start(bf16[256,512]{1,0:T(8,128)(2,1)} %param.23) | copy-start | bytes 786436
  44.6 53.5 %reduce-scatter.3.cloned.1.call-start = ((), (), s32[]{:S(2)}) async-start(), calls=%async_computation.3 | async-start | bytes 2621440 | tf_op jit(solution)/shard_map/reduce_scatter | solution.py:95
  64.8 1.9 copy-start.2
  64.8 2.1 copy-start.5
  66.5 31.6 %copy-start.8 = (f32[128]{0:T(128)S(1)}, f32[128]{0:T(128)}, u32[]{:S(2)}) copy-start(f32[128]{0:T(128)} %param.24) | copy-start | bytes 1540
  66.6 50.7 %all-gather.5.cloned.1.call-start = ((), (), s32[]{:S(2)}) async-start(), calls=%async_computation.4 | async-start | bytes 1310720 | tf_op jit(solution)/shard_map/all_gather | solution.py:103
  100.1 74.6 %all-reduce.6.cloned.1.call-start = ((), (), s32[]{:S(2)}) async-start(), calls=%async_computation.6 | async-start | bytes 2097152 | tf_op jit(solution)/shard_map/psum | solution.py:172
  117.2 2.6 copy-start.1
  117.2 2.6 copy-start.4
  119.9 1.2 copy-start.3
  122.4 85.5 %reduce-scatter.5.cloned.1.call-start = ((), (), s32[]{:S(2)}) async-start(), calls=%async_computation.5 | async-start | bytes 2621440 | tf_op jit(solution)/shard_map/reduce_scatter | solution.py:115
  248.4 7.8 %collective-permute-start.2 = (f32[128,3,134]{0,2,1:T(8,128)S(1)}, f32[128,3,134]{0,2,1:T(8,128)S(1)}, u32[]{:S(2)}, u32[]{:S(2)}) collective-permute-start(f32[128,3,134]{0,2,1:T(8,128)S(1)} %get-tuple-element.111), channel_id=1, source_target_pairs={{0,4},{4,8},{8,12},{12,0},{1,5},{5,9},{9,13},{13,1},{2,6},{6,10},{... | collective-permute-start | bytes 617480 | tf_op jit(solution)/shard_map/ppermute | solution.py:27
  248.5 8.2 %collective-permute-start.3 = (f32[128,3,134]{0,2,1:T(8,128)S(1)}, f32[128,3,134]{0,2,1:T(8,128)S(1)}, u32[]{:S(2)}, u32[]{:S(2)}) collective-permute-start(f32[128,3,134]{0,2,1:T(8,128)S(1)} %get-tuple-element.110), channel_id=1, source_target_pairs={{0,12},{4,0},{8,4},{12,8},{1,13},{5,1},{9,5},{13,9},{2,14},{6,2},{... | collective-permute-start | bytes 617480 | tf_op jit(solution)/shard_map/ppermute | solution.py:27
Sparse Core Ops, SparseCore 0:
  44.7 17.3 all-gather.2
  66.7 31.4 reduce-scatter.2
  100.4 16.8 all-gather.4
  122.5 52.1 all-reduce.5
  177.1 30.7 reduce-scatter.4
where the time goes:
time: 278 us
  waiting for transfers between devices  151 us (54%)
  blocking collectives  57.9 us (21%)
  other arithmetic  27.7 us (10%)
  between operations  14.8 us (5%)
  matrix products  10.7 us (4%)
  starting transfers between devices  7.95 us (3%)
  local copies, waits for them, and re-layouts  7.65 us (3%)
    psum x1, waiting for transfers between devices, body(): lax.psum((kernel_grad, gw_in, gw_out), 'lon')  49.6 us
    reduce_scatter x1, waiting for transfers between devices, body(): lax.psum_scatter(lax.dot_general(w_rows, activated, (((0,), (1,)), ((), (...  31 us
    reduce_scatter x1, waiting for transfers between devices, body(): lax.psum_scatter(lax.dot_general(w_rows, hidden_grad, (((1,), (1,)), ((),...  29.4 us
    psum x1, blocking collectives, body(): lax.psum((kernel_grad, gw_in, gw_out), 'lon')  19.3 us
    all_gather x1, waiting for transfers between devices, body(): normed_all = lax.all_gather(normed, 'ch', axis=0, tiled=True)  17.4 us
    all_gather x1, waiting for transfers between devices, body(): grads_all = lax.all_gather(scaled_grad, 'ch', axis=0, tiled=True)  17 us
    all_gather x1, blocking collectives, body(): top_all = lax.all_gather(top_rows, 'lon', axis=1, tiled=True)  13.6 us
    all_gather x1, blocking collectives, body(): fold_all = lax.all_gather(fold_grad, 'lon', axis=1, tiled=True)  13.1 us
  transfers between devices with their start and end apart: 9, of which 9 were waited for; matrix products, arithmetic and copies ran while one was open for 3% of the time, Pallas kernels for 0%

commit v1 on v0

v1 whole, which is shorter than its diff:
```python
import functools
import math

import jax
import jax.numpy as jnp
from jax import lax
from jax.experimental import pallas as pl
from jax.experimental.pallas import tpu as pltpu
from jax.sharding import PartitionSpec as P

EPSILON = 1e-06
F32 = jnp.float32
BF16 = jnp.bfloat16
MESH = pl.DeviceIdType.MESH
VMEM_SPEC = pl.BlockSpec(memory_space=pltpu.VMEM)
SMEM_SPEC = pl.BlockSpec(memory_space=pltpu.SMEM)
LIMIT = 48 * 1024 * 1024


def greet(axes):
    barrier = pltpu.get_barrier_semaphore()
    total = 0
    for axis in axes:
        count = lax.axis_size(axis)
        me = lax.axis_index(axis)
        for d in range(1, count):
            pl.semaphore_signal(
                barrier, inc=1, device_id={axis: lax.rem(me + d, count)}, device_id_type=MESH
            )
        total += count - 1
    pl.semaphore_wait(barrier, total)


def push(src, dst, sems, slot, axis, target):
    copy = pltpu.make_async_remote_copy(
        src_ref=src,
        dst_ref=dst,
        send_sem=sems[0].at[slot],
        recv_sem=sems[1].at[slot],
        device_id={axis: target},
        device_id_type=MESH,
    )
    copy.start()
    return copy


def edge_kernel(tiles, with_extra, *refs):
    if with_extra:
        x_ref, extra_ref, west_ref, east_ref, tops_ref, extras_ref, send, recv = refs
    else:
        x_ref, west_ref, east_ref, tops_ref, send, recv = refs
    me = lax.axis_index("lon")
    cols, rows = x_ref.shape[0], x_ref.shape[1]
    sems = (send, recv)
    greet(("lon",))
    right, left = lax.rem(me + 1, tiles), lax.rem(me + tiles - 1, tiles)
    copies = [
        push(x_ref.at[pl.ds(cols - 3, 3)], west_ref, sems, 0, "lon", right),
        push(x_ref.at[pl.ds(0, 3)], east_ref, sems, 1, "lon", left),
    ]
    for d in range(1, tiles):
        t = lax.rem(me + d, tiles)
        copies.append(
            push(x_ref.at[:, pl.ds(rows - 16, 16)], tops_ref.at[me], sems, 1 + d, "lon", t)
        )
        if with_extra:
            copies.append(push(extra_ref, extras_ref.at[me], sems, tiles + d, "lon", t))
    tops_ref[me] = x_ref[:, rows - 16 :]
    if with_extra:
        extras_ref[me] = extra_ref[...]
    for copy in copies:
        copy.wait()


def edges(x, extra, collective_id):
    cols, rows, chans = x.shape
    tiles = lax.axis_size("lon")
    out = [
        jax.ShapeDtypeStruct((3, rows, chans), BF16),
        jax.ShapeDtypeStruct((3, rows, chans), BF16),
        jax.ShapeDtypeStruct((tiles, cols, 16, chans), BF16),
    ]
    args = [x]
    if extra is not None:
        out.append(jax.ShapeDtypeStruct((tiles,) + extra.shape, F32))
        args.append(extra)
    return pl.pallas_call(
        functools.partial(edge_kernel, tiles, extra is not None),
        out_shape=out,
        in_specs=[VMEM_SPEC] * len(args),
        out_specs=[VMEM_SPEC] * len(out),
        scratch_shapes=[
            pltpu.SemaphoreType.DMA((2 * tiles + 1,)),
            pltpu.SemaphoreType.DMA((2 * tiles + 1,)),
        ],
        compiler_params=pltpu.CompilerParams(
            collective_id=collective_id, has_side_effects=True, vmem_limit_bytes=LIMIT
        ),
    )(*args)


def fill_shifts(ext_ref, shifts_ref, rows):
    def one(q, _):
        for b in range(7):
            shifts_ref[b, q] = ext_ref[q, pl.ds(5 + b, rows)]
        return 0

    lax.fori_loop(0, ext_ref.shape[0], one, 0)


def conv_kernel(tiles, mine_ref, partner_ref, x_ref, west_ref, east_ref, tops_ref, tap_ref,
                mix_ref, ext_ref, shifts_ref):
    cols, rows, chans = x_ref.shape
    me = mine_ref[0]
    ext_ref[...] = jnp.zeros_like(ext_ref)
    for q in range(cols + 6):
        if q < 3:
            main = west_ref[q]
        elif q < cols + 3:
            main = x_ref[q - 3]
        else:
            main = east_ref[q - cols - 3]
        ext_ref[q, pl.ds(8, rows)] = main.astype(F32)
        step, col = (q - 3) // cols, (q - 3) % cols
        tile = lax.rem(me + step + tiles, tiles)
        top = tops_ref[partner_ref[tile], cols - 1 - col].astype(F32)
        for k in range(3):
            ext_ref[q, pl.ds(8 + rows + k, 1)] = top[15 - k : 16 - k]
    fill_shifts(ext_ref, shifts_ref, rows)

    def one(i, _):
        acc = jnp.zeros((rows, chans), F32)
        for a in range(7):
            for b in range(7):
                acc = acc + tap_ref[pl.ds(a * 7 + b, 1)] * shifts_ref[b, i + a]
        mix_ref[i] = acc
        return 0

    lax.fori_loop(0, cols, one, 0)


def tap_grad_kernel(ext_ref, mg_ref, out_ref, half_ref, shifts_ref, sums_ref):
    cols, rows, chans = mg_ref.shape
    fill_shifts(ext_ref, shifts_ref, rows)
    sums_ref[...] = jnp.zeros_like(sums_ref)
    out_ref[...] = jnp.zeros_like(out_ref)

    def one(i, _):
        mg = mg_ref[i]
        half_ref[i] = mg.astype(BF16)
        for a in range(7):
            for b in range(7):
                prod = shifts_ref[b, i + a] * mg
                sums_ref[a * 7 + b] += jnp.sum(prod.reshape(rows // 8, 8, chans), axis=0)
        return 0

    lax.fori_loop(0, cols, one, 0)
    for t in range(49):
        out_ref[pl.ds(t, 1)] = jnp.sum(sums_ref[t], axis=0, keepdims=True)


def spread_kernel(tiles, mine_ref, partner_ref, mg_ref, west_ref, east_ref, tops_ref, tap_ref,
                  extras_ref, out_ref, kernel_ref, ext_ref, shifts_ref, fold_ref):
    cols, rows, chans = mg_ref.shape
    me = mine_ref[0]
    facing = partner_ref[me]
    ext_ref[...] = jnp.zeros_like(ext_ref)
    fold_ref[...] = jnp.zeros_like(fold_ref)
    for q in range(cols + 6):
        if q < 3:
            main = west_ref[q].astype(F32)
        elif q < cols + 3:
            main = mg_ref[q - 3]
        else:
            main = east_ref[q - cols - 3].astype(F32)
        ext_ref[q, pl.ds(8, rows)] = main
        step, col = (q - 3) // cols, (q - 3) % cols
        tile = lax.rem(facing + step + tiles, tiles)
        top = tops_ref[tile, col].astype(F32)
        for s in range(3):
            for k in range(3 - s):
                fold_ref[s, q, pl.ds(5 + s + k, 1)] = top[15 - k : 16 - k]
    fill_shifts(ext_ref, shifts_ref, rows)

    def one(i, _):
        acc = jnp.zeros((rows, chans), F32)
        for a in range(7):
            for b in range(7):
                acc = acc + tap_ref[pl.ds(a * 7 + b, 1)] * shifts_ref[6 - b, i + 6 - a]
        out_ref[i] = acc
        north = jnp.zeros((8, chans), F32)
        for a in range(7):
            for s in range(3):
                north = north + tap_ref[pl.ds(a * 7 + 6 - s, 1)] * fold_ref[
                    s, cols - 1 - i + 6 - a
                ]
        out_ref[i, pl.ds(rows - 8, 8)] += north
        return 0

    lax.fori_loop(0, cols, one, 0)
    kernel_ref[...] = jnp.sum(extras_ref[...], axis=0)


def gelu_parts(hidden):
    normal_cdf = 0.5 * (1.0 + lax.erf(hidden * (1.0 / math.sqrt(2.0))))
    density = jnp.exp(-0.5 * hidden * hidden) * (1.0 / math.sqrt(2.0 * math.pi))
    return (hidden * normal_cdf, normal_cdf + hidden * density)


def dot(a, b, dims):
    return lax.dot_general(a, b, (dims, ((), ())), preferred_element_type=F32)


def middle_kernel(n, tiles, factor, block,
                  mix_ref, sg_ref, win_ref, wout_ref, gain_ref, shift_ref,
                  branch_ref, mg_ref, gwin_ref, gwout_ref,
                  mixg, normed, act, agrad, hg, mean, inv, own_ng, one_acc, two_acc,
                  nsend, nrecv, bsend, brecv, psend, precv,
                  gof, gsi, gri, agi, gso, gro, ago,
                  *sem_refs):
    cells, chans = mix_ref.shape
    hid = win_ref.shape[2]
    width = n * chans
    blocks = cells // block
    m_sems, n_sems, p_sems, b_sems, i_sems, o_sems, ai_sems, ao_sems = [
        (sem_refs[2 * k], sem_refs[2 * k + 1]) for k in range(8)
    ]
    me = lax.axis_index("ch")
    lon = lax.axis_index("lon")
    greet(("ch", "lon"))
    peers = [lax.rem(me + d, n) for d in range(n)]
    spans = [lax.rem(lon + d, tiles) for d in range(tiles)]

    def loop(step):
        def one(i, _):
            step(pl.ds(pl.multiple_of(i * block, block), block))
            return 0

        lax.fori_loop(0, blocks, one, 0)

    mixg[me] = mix_ref[...].astype(BF16)
    copies = [
        push(mixg.at[me], mixg.at[me], m_sems, d, "ch", peers[d]) for d in range(1, n)
    ]

    def grads(rows):
        total = dot(sg_ref[0, rows], wout_ref[0], ((1,), (1,)))
        for j in range(1, n):
            total = total + dot(sg_ref[j, rows], wout_ref[j], ((1,), (1,)))
        agrad[rows] = total

    loop(grads)
    for copy in copies:
        copy.wait()

    def forward(rows):
        parts = [mixg[j, rows].astype(F32) for j in range(n)]
        one = functools.reduce(jnp.add, parts)
        two = functools.reduce(jnp.add, [v * v for v in parts])
        mean_cell = jnp.sum(one, axis=1, keepdims=True) / width
        sigma = lax.rsqrt(
            jnp.sum(two, axis=1, keepdims=True) / width - mean_cell * mean_cell + EPSILON
        )
        mean[rows] = mean_cell
        inv[rows] = sigma
        hidden = jnp.zeros((block, hid), F32)
        for j in range(n):
            value = ((parts[j] - mean_cell) * sigma * gain_ref[j] + shift_ref[j]).astype(BF16)
            normed[j, rows] = value
            hidden = hidden + dot(value, win_ref[j], ((1,), (0,)))
        activation, slope = gelu_parts(hidden)
        act[rows] = activation.astype(BF16)
        hg[rows] = (agrad[rows] * slope).astype(BF16)
        one_acc[rows] = jnp.zeros((block, chans), F32)
        two_acc[rows] = jnp.zeros((block, chans), F32)

    loop(forward)

    ncopies = []
    for d in list(range(1, n)) + [0]:
        t = peers[d]

        def back(rows, d=d, t=t):
            part = dot(hg[rows], win_ref[t], ((1,), (1,)))
            if d:
                nsend[d, rows] = part.astype(BF16)
            else:
                own_ng[rows] = part
            scaled = part * gain_ref[t]
            centred = (mixg[t, rows].astype(F32) - mean[rows]) * inv[rows]
            one_acc[rows] += scaled
            two_acc[rows] += scaled * centred

        loop(back)
        if d:
            ncopies.append(push(nsend.at[d], nrecv.at[d], n_sems, d, "ch", t))
    lane = lax.broadcasted_iota(jnp.int32, (cells, 128), 1)
    pair = jnp.where(
        lane == 0,
        jnp.sum(one_acc[...], axis=1, keepdims=True),
        jnp.sum(two_acc[...], axis=1, keepdims=True),
    )
    psend[...] = pair.T[:8]
    pcopies = [push(psend, precv.at[d], p_sems, d, "ch", peers[d]) for d in range(1, n)]

    for j in range(n):
        part = dot(act[...], sg_ref[j], ((0,), (0,)))
        gof[pl.ds(j * hid, hid)] = part
        gso[pl.ds(j * hid, hid)] = part.astype(BF16)
    ro, ri = n * hid // tiles, width // tiles
    rcopies = []
    for d in range(1, tiles):
        src = gso.at[pl.ds(pl.multiple_of(spans[d] * ro, ro), ro)]
        rcopies.append(push(src, gro.at[d], o_sems, d, "lon", spans[d]))
    for j in range(n):
        part = dot(normed[j], hg[...], ((0,), (0,)))
        gwin_ref[pl.ds(j * chans, chans)] = part
        gsi[pl.ds(j * chans, chans)] = part.astype(BF16)
    for d in range(1, tiles):
        src = gsi.at[pl.ds(pl.multiple_of(spans[d] * ri, ri), ri)]
        rcopies.append(push(src, gri.at[d], i_sems, d, "lon", spans[d]))

    bcopies = []
    for d in range(1, n):
        t = peers[d]

        def out(rows, d=d, t=t):
            bsend[d, rows] = dot(act[rows], wout_ref[t], ((1,), (0,))).astype(BF16)

        loop(out)
        bcopies.append(push(bsend.at[d], brecv.at[d], b_sems, d, "ch", t))

    def out_own(rows):
        branch_ref[rows] = dot(act[rows], wout_ref[me], ((1,), (0,)))

    loop(out_own)

    for copy in rcopies:
        copy.wait()
    own_o = gof[pl.ds(pl.multiple_of(lon * ro, ro), ro)]
    own_i = gwin_ref[pl.ds(pl.multiple_of(lon * ri, ri), ri)]
    for d in range(1, tiles):
        own_o = own_o + gro[d].astype(F32)
        own_i = own_i + gri[d].astype(F32)
    ago[lon] = (own_o * factor).astype(BF16)
    agi[lon] = (own_i * factor).astype(BF16)
    acopies = []
    for d in range(1, tiles):
        acopies.append(push(ago.at[lon], ago.at[lon], ao_sems, d, "lon", spans[d]))
        acopies.append(push(agi.at[lon], agi.at[lon], ai_sems, d, "lon", spans[d]))

    for copy in pcopies + ncopies:
        copy.wait()
    sums = psend[...]
    for d in range(1, n):
        sums = sums + precv[d]
    cols = jnp.concatenate([sums, jnp.zeros((120, cells), F32)], axis=0).T
    one_acc_mean = cols[:, 0:1] / width
    mean_two = cols[:, 1:2] / width
    total = own_ng[...]
    for d in range(1, n):
        total = total + nrecv[d].astype(F32)
    centred = (mix_ref[...] - mean[...]) * inv[...]
    mg_ref[...] = inv[...] * (total * gain_ref[me] - one_acc_mean - centred * mean_two)

    for copy in bcopies:
        copy.wait()
    total = branch_ref[...]
    for d in range(1, n):
        total = total + brecv[d].astype(F32)
    branch_ref[...] = total
    for copy in acopies:
        copy.wait()
    for t in range(tiles):
        gwin_ref[pl.ds(t * ri, ri)] = agi[t].astype(F32)
        for u in range(t * ro, (t + 1) * ro, min(ro, hid)):
            size = min(ro, hid)
            j, f = u // hid, u % hid
            gwout_ref[pl.ds(f, size), pl.ds(j * chans, chans)] = ago[
                t, pl.ds(u - t * ro, size)
            ].astype(F32)


def middle(mix, sg_all, win, wout, gain, shift, factor):
    cells, chans = mix.shape
    n, _, hid = win.shape
    tiles = lax.axis_size("lon")
    width = n * chans
    ro, ri = n * hid // tiles, width // tiles
    S = pltpu.VMEM
    scratch = [
        S((n, cells, chans), BF16), S((n, cells, chans), BF16),
        S((cells, hid), BF16), S((cells, hid), F32), S((cells, hid), BF16),
        S((cells, 1), F32), S((cells, 1), F32), S((cells, chans), F32),
        S((cells, chans), F32), S((cells, chans), F32),
        S((n, cells, chans), BF16), S((n, cells, chans), BF16),
        S((n, cells, chans), BF16), S((n, cells, chans), BF16),
        S((8, cells), F32), S((n, 8, cells), F32),
        S((n * hid, chans), F32),
        S((width, hid), BF16), S((tiles, ri, hid), BF16), S((tiles, ri, hid), BF16),
        S((n * hid, chans), BF16), S((tiles, ro, chans), BF16), S((tiles, ro, chans), BF16),
    ]
    for count in (n, n, n, n, tiles, tiles, tiles, tiles):
        scratch += [pltpu.SemaphoreType.DMA((count,)), pltpu.SemaphoreType.DMA((count,))]
    return pl.pallas_call(
        functools.partial(middle_kernel, n, tiles, factor, 256),
        out_shape=[
            jax.ShapeDtypeStruct((cells, chans), F32),
            jax.ShapeDtypeStruct((cells, chans), F32),
            jax.ShapeDtypeStruct((width, hid), F32),
            jax.ShapeDtypeStruct((hid, width), F32),
        ],
        in_specs=[VMEM_SPEC] * 6,
        out_specs=[VMEM_SPEC] * 4,
        scratch_shapes=scratch,
        compiler_params=pltpu.CompilerParams(
            collective_id=1, has_side_effects=True, vmem_limit_bytes=LIMIT
        ),
    )(mix, sg_all, win, wout, gain, shift)


def body(
    field_in, sea_mask, fold_partner, kernel, ln_gain, ln_shift, w_in, w_out, layer_scale, grad_out
):
    chans, cols, rows = field_in.shape
    tiles = lax.axis_size("lon")
    n = lax.axis_size("ch")
    cells = cols * rows
    hid = w_in.shape[1]
    mine = lax.axis_index("lon").astype(jnp.int32).reshape(1)
    factor = 1.0 / math.sqrt(tiles * cells)
    plain = pltpu.CompilerParams(vmem_limit_bytes=LIMIT)

    ocean_f = sea_mask.astype(F32)[None]
    masked = (field_in * sea_mask.astype(BF16)[None]).transpose(1, 2, 0)
    grad_f = grad_out.astype(F32)
    scaled_grad = (
        (ocean_f * layer_scale[:, None, None] * grad_f)
        .astype(BF16)
        .transpose(1, 2, 0)
        .reshape(cells, chans)
    )
    sg_all = lax.all_gather(scaled_grad, "ch", axis=0, tiled=False)
    taps = jnp.pad(kernel.reshape(chans, 49).T, ((0, 7), (0, 0)))

    west, east, tops = edges(masked, None, 0)
    mix, ext = pl.pallas_call(
        functools.partial(conv_kernel, tiles),
        out_shape=[
            jax.ShapeDtypeStruct((cols, rows, chans), F32),
            jax.ShapeDtypeStruct((cols + 6, rows + 16, chans), F32),
        ],
        in_specs=[SMEM_SPEC, SMEM_SPEC] + [VMEM_SPEC] * 5,
        out_specs=[VMEM_SPEC] * 2,
        scratch_shapes=[pltpu.VMEM((7, cols + 6, rows, chans), F32)],
        compiler_params=plain,
    )(mine, fold_partner, masked, west, east, tops, taps)

    branch, mg, gw_in, gw_out = middle(
        mix.reshape(cells, chans),
        sg_all,
        w_in.reshape(n, chans, hid),
        w_out.reshape(hid, n, chans).transpose(1, 0, 2),
        ln_gain.reshape(n, 1, chans),
        ln_shift.reshape(n, 1, chans),
        factor,
    )
    mg = mg.reshape(cols, rows, chans)
    tap_sums, half = pl.pallas_call(
        tap_grad_kernel,
        out_shape=[
            jax.ShapeDtypeStruct((56, chans), F32),
            jax.ShapeDtypeStruct((cols, rows, chans), BF16),
        ],
        in_specs=[VMEM_SPEC] * 2,
        out_specs=[VMEM_SPEC] * 2,
        scratch_shapes=[
            pltpu.VMEM((7, cols + 6, rows, chans), F32),
            pltpu.VMEM((49, 8, chans), F32),
        ],
        compiler_params=plain,
    )(ext, mg)
    west, east, tops, extras = edges(half, tap_sums, 2)
    field_grad, kernel_total = pl.pallas_call(
        functools.partial(spread_kernel, tiles),
        out_shape=[
            jax.ShapeDtypeStruct((cols, rows, chans), F32),
            jax.ShapeDtypeStruct((56, chans), F32),
        ],
        in_specs=[SMEM_SPEC, SMEM_SPEC] + [VMEM_SPEC] * 6,
        out_specs=[VMEM_SPEC] * 2,
        scratch_shapes=[
            pltpu.VMEM((cols + 6, rows + 16, chans), F32),
            pltpu.VMEM((7, cols + 6, rows, chans), F32),
            pltpu.VMEM((3, cols + 6, 8, chans), F32),
        ],
        compiler_params=plain,
    )(mine, fold_partner, mg, west, east, tops, taps, extras)

    block_out = (
        ocean_f
        * (
            field_in.astype(F32)
            + layer_scale[:, None, None] * branch.T.reshape(chans, cols, rows)
        )
    ).astype(BF16)
    grad_x = (ocean_f * (grad_f + field_grad.transpose(2, 0, 1))).astype(BF16)
    kernel_grad = kernel_total[:49].T.reshape(chans, 7, 7) * factor
    return (block_out, grad_x, kernel_grad, gw_in, gw_out)


def solution(mesh):
    placed = (
        P("ch", ("grp", "lon"), None),
        P("lon", None),
        P(),
        P("ch", None, None),
        P(),
        P(),
        P(None, "ch"),
        P("ch", None),
        P("ch"),
        P("ch", ("grp", "lon"), None),
    )
    return jax.shard_map(
        body,
        mesh=mesh,
        in_specs=placed,
        out_specs=(
            P("ch", ("grp", "lon"), None),
            P("ch", ("grp", "lon"), None),
            P(("grp", "ch"), None, None),
            P("grp", "ch"),
            P(("grp", "ch"), None),
        ),
        check_vma=False,
    )
```

time: 278 us -> 109 us (0.39)
  waiting for transfers between devices: 151 us -> 0.41 us
  Pallas kernels: 0 us -> 80.8 us
  blocking collectives: 57.9 us -> 0 us
  other arithmetic: 27.7 us -> 2.14 us
  matrix products: 10.7 us -> 0 us
  starting transfers between devices: 7.95 us -> 0.04 us
  local copies, waits for them, and re-layouts: 7.65 us -> 10.9 us
    pallas_call x0 -> x6, Pallas kernels: none -> 80.8 us  [the longest x1 45.2 us: middle(): pl.pallas_call(functools.partial(middle_kernel, n, tiles, factor, 256), o...]
    reduce_scatter x2 -> x0, waiting for transfers between devices: 60.5 us -> none  [the longest x1 31 us: body(): lax.psum_scatter(lax.dot_general(w_rows, activated, (((0,), (1,)), ((), (...]
    psum x1 -> x0, waiting for transfers between devices: 49.6 us -> none  [body(): lax.psum((kernel_grad, gw_in, gw_out), 'lon')]
    all_gather x2 -> x1, waiting for transfers between devices: 34.5 us -> 0.4 us  [body(): sg_all = lax.all_gather(scaled_grad, 'ch', axis=0, tiled=False)]
    psum x3 -> x0, blocking collectives: 31.3 us -> none  [the longest x1 19.3 us: body(): lax.psum((kernel_grad, gw_in, gw_out), 'lon')]
    all_gather x2 -> x0, blocking collectives: 26.7 us -> none  [the longest x1 13.6 us: body(): top_all = lax.all_gather(top_rows, 'lon', axis=1, tiled=True)]
    reduce_sum x6 -> x0, other arithmetic: 10.9 us -> none  [the longest x3 4.08 us: body(): jnp.sum(extended_f[:, row_tap:row_tap + lon_dev, col_tap:col_tap + lat_co...]
    dot_general x6 -> x0, matrix products: 10.7 us -> none  [the longest x1 2.64 us: body(): lax.dot_general(normed_all, w_in, (((0,), (0,)), ((), ())), preferred_ele...]
  transfers between devices with their start and end apart: 9 -> 1, of which waited for: 9 -> 1; matrix products, arithmetic and copies ran while one was open for 3% -> 1% of each run, Pallas kernels for 0% -> 14%
where the time goes in v1:
time: 109 us; the launch traced here: 108 us
  Pallas kernels  80.8 us (74%)
  between operations  14.2 us (13%)
  local copies, waits for them, and re-layouts  10.9 us (10%)
  other arithmetic  2.14 us (2%)
    pallas_call x1, Pallas kernels, middle(): pl.pallas_call(functools.partial(middle_kernel, n, tiles, factor, 256), o...  45.2 us
    pallas_call x2, Pallas kernels, edges(): pl.pallas_call(functools.partial(edge_kernel, tiles, extra is not None),...  27 us
    unnamed x29, local copies, waits for them, and re-layouts  10.1 us
    pallas_call x1, Pallas kernels, body(): pl.pallas_call(functools.partial(conv_kernel, tiles), out_shape=[jax.Shap...  3.14 us
    pallas_call x1, Pallas kernels, body(): pl.pallas_call(functools.partial(spread_kernel, tiles), out_shape=[jax.Sh...  2.94 us
    pallas_call x1, Pallas kernels, body(): pl.pallas_call(tap_grad_kernel, out_shape=[jax.ShapeDtypeStruct((56, chan...  2.43 us
  transfers between devices with their start and end apart: 1, of which 1 were waited for; matrix products, arithmetic and copies ran while one was open for 1% of the time, Pallas kernels for 14%

profile of v1, /device:TPU:0, one launch (start us, length us, event | category | flops | bytes accessed | tf_op | source)
XLA Modules:
  0.0 108.4 jit_solution(7555318723067952335)
XLA Ops:
  7.2 0.0 all-gather.2.cloned.1.call-start
  7.2 0.8 fusion.3
  8.0 1.1 %copy.29 = bf16[128,8,128]{0,2,1:T(8,128)(2,1)S(1)} copy(bf16[128,8,128]{2,1,0:T(8,128)(2,1)} %param.19) | data formatting | bytes 524288 | tf_op args[9]
  9.1 0.0 copy-start.10
  9.1 0.6 copy-done.10
  9.8 0.0 copy-start.9
  9.8 0.9 fusion
  10.7 0.0 copy-start.7
  10.7 0.0 all-gather.2.cloned.1.call-update
  10.7 0.0 copy-done.9
  10.7 0.9 copy-done.7
  11.6 0.0 copy-start.8
  11.6 0.2 copy.27
  11.9 0.7 copy-done.8
  12.6 0.0 copy-start.5
  12.6 0.1 copy.30
  12.7 0.2 copy.31
  12.9 0.4 copy-done.5
  13.3 0.2 multiply_bitcast_fusion.refs_0_.x_ref
  13.5 12.6 %shard_map.137 = (bf16[3,128,128]{2,1,0:T(8,128)(2,1)S(1)}, bf16[3,128,128]{2,1,0:T(8,128)(2,1)S(1)}, bf16[4,8,16,128]{3,2,1,0:T(8,128)(2,1)S(1)}) custom-call(bf16[8,128,128]{2,1,0:T(8,128)(2,1)S(1)} %multiply_bitcast_fusion.refs_0_.x_ref), custom_call_target="tpu_custom_call" | custom-call | tf_op jit(solution)/shard_map/pallas_call | solution.py:87
  26.1 0.0 copy-start.2
  26.1 0.6 copy-done.2
  26.8 0.0 copy-start.1
  26.8 3.1 %shard_map.138 = (f32[8,128,128]{2,1,0:T(8,128)S(1)}, f32[14,144,128]{2,1,0:T(8,128)S(1)}) custom-call(s32[1]{0:T(128)} %bitcast.mine_ref, s32[4]{0:T(128)S(1)} %copy-done.2, bf16[8,128,128]{2,1,0:T(8,128)(2,1)S(1)} %multiply_bitcast_fusion.refs_0_.x_ref, bf16[3,128,128]{2,1,0:T(8,128)(2,1)S(1)} %get-tuple-element.22.west_ref, ...), custom_call_target="tpu_custom_call" | custom-call | tf_op jit(solution)/shard_map/pallas_call | solution.py:447
  29.9 0.4 all-gather.2.cloned.1.call-done.sg_ref
  30.3 0.0 copy-start.4
  30.3 0.0 copy-start.3
  30.3 0.0 copy-done.1
  30.3 0.7 copy-done.4
  31.0 0.0 copy-done.3
  31.0 0.0 copy-start
  31.0 1.2 %copy-done = bf16[4,1024,128]{2,1,0:T(8,128)(2,1)S(1)} copy-done((bf16[4,1024,128]{2,1,0:T(8,128)(2,1)S(1)}, bf16[4,1024,128]{2,1,0:T(8,128)(2,1)}, u32[]{:S(2)}) %copy-start) | copy-done | bytes 1048600
  32.2 45.2 %shard_map.139 = (f32[1024,128]{1,0:T(8,128)S(1)}, f32[1024,128]{1,0:T(8,128)S(1)}, f32[512,256]{1,0:T(8,128)S(1)}, f32[256,512]{1,0:T(8,128)S(1)}) custom-call(f32[1024,128]{1,0:T(8,128)S(1)} %bitcast.29, bf16[4,1024,128]{2,1,0:T(8,128)(2,1)S(1)} %copy-done, bf16[4,128,256]{2,1,0:T(8,128)(2,1)S(1)} %bitcast.30, bf16[4,256,128]{2,1,0:T(8,128)(2,1)S(1)} %bitcast.27, ...), custom_call_target="tpu_custom_call" | custom-call | tf_op jit(solution)/shard_map/pallas_call | solution.py:405
  77.5 2.4 %shard_map.140 = (f32[56,128]{1,0:T(8,128)S(1)}, bf16[8,128,128]{2,1,0:T(8,128)(2,1)S(1)}) custom-call(f32[14,144,128]{2,1,0:T(8,128)S(1)} %get-tuple-element.28.ext_ref, f32[8,128,128]{2,1,0:T(8,128)S(1)} %bitcast.25), custom_call_target="tpu_custom_call" | custom-call | tf_op jit(solution)/shard_map/pallas_call | solution.py:469
  79.9 14.5 %shard_map.141 = (bf16[3,128,128]{2,1,0:T(8,128)(2,1)S(1)}, bf16[3,128,128]{2,1,0:T(8,128)(2,1)S(1)}, bf16[4,8,16,128]{3,2,1,0:T(8,128)(2,1)S(1)}, f32[4,56,128]{2,1,0:T(8,128)S(1)}) custom-call(bf16[8,128,128]{2,1,0:T(8,128)(2,1)S(1)} %get-tuple-element.29.refs_0_, f32[56,128]{1,0:T(8,128)S(1)} %get-tuple-element.30.refs_1_), custom_call_target="tpu_custom_call" | custom-call | tf_op jit(solution)/shard_map/pallas_call | solution.py:87
  94.4 0.0 copy-start.6
  94.4 2.9 %shard_map.142 = (f32[8,128,128]{2,1,0:T(8,128)S(1)}, f32[56,128]{1,0:T(8,128)S(1)}) custom-call(s32[1]{0:T(128)} %bitcast.mine_ref, s32[4]{0:T(128)S(1)} %copy-done.2, f32[8,128,128]{2,1,0:T(8,128)S(1)} %bitcast.26, bf16[3,128,128]{2,1,0:T(8,128)(2,1)S(1)} %get-tuple-element.31.west_ref, bf16[3,128,128]{2,1,0:T(8,128)(2,1)S(1)} %get-tuple-element.32.east_ref, ...), custom_call_target="tpu_custom_call" | custom-call | tf_op jit(solution)/shard_map/pallas_call | solution.py:484
  97.3 0.0 copy-done.6
  97.3 0.3 fusion.2
  97.6 0.9 copy.33
  98.5 0.6 mul.66
  99.1 0.9 copy.32
  100.0 0.8 copy.36
  100.8 0.8 copy.37
  (3 shorter events, 0.0 us)
Async XLA Ops:
  7.2 23.1 %all-gather.2.cloned.1.call-start = ((), (), s32[]{:S(2)}) async-start(), calls=%async_computation | async-start | bytes 1310720 | tf_op jit(solution)/shard_map/all_gather | solution.py:443
  9.1 0.7 copy-start.10
  9.8 0.9 copy-start.9
  10.7 0.9 copy-start.7
  11.6 0.9 copy-start.8
  12.6 0.7 copy-start.5
  26.1 0.7 copy-start.2
  26.8 3.5 %copy-start.1 = (bf16[512,256]{1,0:T(8,128)(2,1)S(1)}, bf16[512,256]{1,0:T(8,128)(2,1)}, u32[]{:S(2)}) copy-start(bf16[512,256]{1,0:T(8,128)(2,1)} %param.16) | copy-start | bytes 786436
  30.3 0.7 copy-start.4
  30.3 0.7 copy-start.3
  31.0 1.2 %copy-start = (bf16[4,1024,128]{2,1,0:T(8,128)(2,1)S(1)}, bf16[4,1024,128]{2,1,0:T(8,128)(2,1)}, u32[]{:S(2)}) copy-start(bf16[4,1024,128]{2,1,0:T(8,128)(2,1)} %all-gather.2.cloned.1.call-done.sg_ref) | copy-start | bytes 3145732
  94.4 3.0 %copy-start.6 = (bf16[128,8,128]{0,2,1:T(8,128)(2,1)S(1)}, bf16[128,8,128]{0,2,1:T(8,128)(2,1)}, u32[]{:S(2)}) copy-start(bf16[128,8,128]{0,2,1:T(8,128)(2,1)} %copy-done.5) | copy-start | bytes 786436
Sparse Core Ops, SparseCore 0:
  10.8 19.4 all-gather.1

commit v2 on v1

v2 whole, which is shorter than its diff:
```python
import functools
import math

import jax
import jax.numpy as jnp
from jax import lax
from jax.experimental import pallas as pl
from jax.experimental.pallas import tpu as pltpu
from jax.sharding import PartitionSpec as P

EPSILON = 1e-06
F32 = jnp.float32
BF16 = jnp.bfloat16
MESH = pl.DeviceIdType.MESH
VMEM_SPEC = pl.BlockSpec(memory_space=pltpu.VMEM)
SMEM_SPEC = pl.BlockSpec(memory_space=pltpu.SMEM)
LIMIT = 48 * 1024 * 1024


def greet(axes):
    barrier = pltpu.get_barrier_semaphore()
    total = 0
    for axis in axes:
        count = lax.axis_size(axis)
        me = lax.axis_index(axis)
        for d in range(1, count):
            pl.semaphore_signal(
                barrier, inc=1, device_id={axis: lax.rem(me + d, count)}, device_id_type=MESH
            )
        total += count - 1
    pl.semaphore_wait(barrier, total)


def push(src, dst, sems, slot, axis, target):
    copy = pltpu.make_async_remote_copy(
        src_ref=src,
        dst_ref=dst,
        send_sem=sems[0].at[slot],
        recv_sem=sems[1].at[slot],
        device_id={axis: target},
        device_id_type=MESH,
    )
    copy.start()
    return copy


def gelu_parts(hidden):
    normal_cdf = 0.5 * (1.0 + lax.erf(hidden * (1.0 / math.sqrt(2.0))))
    density = jnp.exp(-0.5 * hidden * hidden) * (1.0 / math.sqrt(2.0 * math.pi))
    return (hidden * normal_cdf, normal_cdf + hidden * density)


def dot(a, b, dims):
    return lax.dot_general(a, b, (dims, ((), ())), preferred_element_type=F32)


def fill_shifts(ext_ref, shifts_ref, rows):
    def one(q, _):
        for b in range(7):
            shifts_ref[b, q] = ext_ref[q, pl.ds(5 + b, rows)]
        return 0

    lax.fori_loop(0, ext_ref.shape[0], one, 0)


def send_edges(x_ref, pack, west, east, tops, sems, me, tiles):
    cols, rows, chans = x_ref.shape
    right, left = lax.rem(me + 1, tiles), lax.rem(me + tiles - 1, tiles)
    copies = [
        push(x_ref.at[pl.ds(cols - 3, 3)], west, sems, 0, "lon", right),
        push(x_ref.at[pl.ds(0, 3)], east, sems, tiles, "lon", left),
    ]
    for col in range(cols):
        top = x_ref[col, pl.ds(rows - 16, 16)].astype(F32)
        for k in range(3):
            pack[pl.ds(col * 3 + k, 1)] = top[15 - k : 16 - k]
    tops[me] = pack[...].astype(BF16)
    for d in range(1, tiles):
        t = lax.rem(me + d, tiles)
        copies.append(push(tops.at[me], tops.at[me], sems, d, "lon", t))
    return copies


def mega_kernel(n, tiles, factor, block,
                partner_ref, x_ref, sg_ref, tap_ref, win_ref, wout_all, gain_ref, shift_ref,
                branch_ref, fg_ref, kernel_ref, agi, ago,
                ext_ref, shifts_ref, fold_ref, pack, west, east, tops, west2, east2, tops2,
                half_ref, sums_ref, extras_ref, extra_ref, wout_ref, mix_ref, sgg,
                mixg, normed, act, agrad, hg, mean, inv, own_ng, one_acc, two_acc,
                nsend, nrecv, bsend, brecv, psend, precv,
                gof, gif, gsi, gri, gso, gro,
                *sem_refs):
    cols, rows, chans = x_ref.shape
    cells = cols * rows
    hid = win_ref.shape[2]
    width = n * chans
    blocks = cells // block
    (m_sems, n_sems, p_sems, b_sems, s_sems, i_sems, o_sems, ai_sems, ao_sems, k_sems,
     e_sems, f_sems) = [(sem_refs[2 * k], sem_refs[2 * k + 1]) for k in range(12)]
    me = lax.axis_index("ch")
    lon = lax.axis_index("lon")
    greet(("ch", "lon"))
    peers = [lax.rem(me + d, n) for d in range(n)]
    spans = [lax.rem(lon + d, tiles) for d in range(tiles)]

    def loop(step):
        def one(i, _):
            step(pl.ds(pl.multiple_of(i * block, block), block))
            return 0

        lax.fori_loop(0, blocks, one, 0)

    pack[...] = jnp.zeros_like(pack)
    ecopies = send_edges(x_ref, pack, west, east, tops, e_sems, lon, tiles)
    scopies = [push(sg_ref, sgg.at[me], s_sems, d, "ch", peers[d]) for d in range(1, n)]
    sgg[me] = sg_ref[...]
    for j in range(n):
        wout_ref[j] = wout_all[:, j * chans : (j + 1) * chans]
    ext_ref[...] = jnp.zeros_like(ext_ref)
    fold_ref[...] = jnp.zeros_like(fold_ref)
    for q in range(cols):
        ext_ref[q + 3, pl.ds(8, rows)] = x_ref[q].astype(F32)
    for copy in ecopies:
        copy.wait()

    for q in range(3):
        ext_ref[q, pl.ds(8, rows)] = west[q].astype(F32)
        ext_ref[cols + 3 + q, pl.ds(8, rows)] = east[q].astype(F32)
    for step in (-1, 0, 1):
        tile = lax.rem(lon + step + tiles, tiles)
        top = tops[partner_ref[tile]].astype(F32)
        for q in range(cols + 6):
            if (q - 3) // cols == step:
                base = (cols - 1 - (q - 3) % cols) * 3
                ext_ref[q, pl.ds(8 + rows, 3)] = top[base : base + 3]
    fill_shifts(ext_ref, shifts_ref, rows)

    def conv(i, _):
        acc = jnp.zeros((rows, chans), F32)
        for a in range(7):
            for b in range(7):
                acc = acc + tap_ref[pl.ds(a * 7 + b, 1)] * shifts_ref[b, i + a]
        cut = pl.ds(pl.multiple_of(i * rows, rows), rows)
        mix_ref[cut] = acc
        mixg[me, cut] = acc.astype(BF16)
        return 0

    lax.fori_loop(0, cols, conv, 0)
    mcopies = [
        push(mixg.at[me], mixg.at[me], m_sems, d, "ch", peers[d]) for d in range(1, n)
    ]
    for copy in scopies:
        copy.wait()

    def grads(cut):
        total = dot(sgg[0, cut], wout_ref[0], ((1,), (1,)))
        for j in range(1, n):
            total = total + dot(sgg[j, cut], wout_ref[j], ((1,), (1,)))
        agrad[cut] = total

    loop(grads)
    for copy in mcopies:
        copy.wait()

    def forward(cut):
        parts = [mixg[j, cut].astype(F32) for j in range(n)]
        one = functools.reduce(jnp.add, parts)
        two = functools.reduce(jnp.add, [v * v for v in parts])
        mean_cell = jnp.sum(one, axis=1, keepdims=True) / width
        sigma = lax.rsqrt(
            jnp.sum(two, axis=1, keepdims=True) / width - mean_cell * mean_cell + EPSILON
        )
        mean[cut] = mean_cell
        inv[cut] = sigma
        hidden = jnp.zeros((block, hid), F32)
        for j in range(n):
            value = ((parts[j] - mean_cell) * sigma * gain_ref[j] + shift_ref[j]).astype(BF16)
            normed[j, cut] = value
            hidden = hidden + dot(value, win_ref[j], ((1,), (0,)))
        activation, slope = gelu_parts(hidden)
        act[cut] = activation.astype(BF16)
        hg[cut] = (agrad[cut] * slope).astype(BF16)
        one_acc[cut] = jnp.zeros((block, chans), F32)
        two_acc[cut] = jnp.zeros((block, chans), F32)

    loop(forward)

    ro, ri = n * hid // tiles, width // tiles
    for j in range(n):
        part = dot(act[...], sgg[j], ((0,), (0,)))
        gof[pl.ds(j * hid, hid)] = part
        gso[pl.ds(j * hid, hid)] = part.astype(BF16)
    ocopies, icopies = [], []
    for d in range(1, tiles):
        src = gso.at[pl.ds(pl.multiple_of(spans[d] * ro, ro), ro)]
        ocopies.append(push(src, gro.at[d], o_sems, d, "lon", spans[d]))

    ncopies = []
    for d in list(range(1, n)) + [0]:
        t = peers[d]

        def back(cut, d=d, t=t):
            part = dot(hg[cut], win_ref[t], ((1,), (1,)))
            if d:
                nsend[d, cut] = part.astype(BF16)
            else:
                own_ng[cut] = part
            scaled = part * gain_ref[t]
            centred = (mixg[t, cut].astype(F32) - mean[cut]) * inv[cut]
            one_acc[cut] += scaled
            two_acc[cut] += scaled * centred

        loop(back)
        if d:
            ncopies.append(push(nsend.at[d], nrecv.at[d], n_sems, d, "ch", t))
    lane = lax.broadcasted_iota(jnp.int32, (cells, 128), 1)
    pair = jnp.where(
        lane == 0,
        jnp.sum(one_acc[...], axis=1, keepdims=True),
        jnp.sum(two_acc[...], axis=1, keepdims=True),
    )
    psend[...] = pair.T[:8]
    pcopies = [push(psend, precv.at[d], p_sems, d, "ch", peers[d]) for d in range(1, n)]

    for j in range(n):
        part = dot(normed[j], hg[...], ((0,), (0,)))
        gif[pl.ds(j * chans, chans)] = part
        gsi[pl.ds(j * chans, chans)] = part.astype(BF16)
    for d in range(1, tiles):
        src = gsi.at[pl.ds(pl.multiple_of(spans[d] * ri, ri), ri)]
        icopies.append(push(src, gri.at[d], i_sems, d, "lon", spans[d]))

    bcopies = []
    for d in range(1, n):
        t = peers[d]

        def out(cut, d=d, t=t):
            bsend[d, cut] = dot(act[cut], wout_ref[t], ((1,), (0,))).astype(BF16)

        loop(out)
        bcopies.append(push(bsend.at[d], brecv.at[d], b_sems, d, "ch", t))

    def out_own(cut):
        branch_ref[cut] = dot(act[cut], wout_ref[me], ((1,), (0,)))

    loop(out_own)

    for copy in pcopies + ncopies:
        copy.wait()
    sums = psend[...]
    for d in range(1, n):
        sums = sums + precv[d]
    both = jnp.concatenate([sums, jnp.zeros((120, cells), F32)], axis=0).T
    one_mean = both[:, 0:1] / width
    two_mean = both[:, 1:2] / width
    total = own_ng[...]
    for d in range(1, n):
        total = total + nrecv[d].astype(F32)
    centred = (mix_ref[...] - mean[...]) * inv[...]
    own_ng[...] = inv[...] * (total * gain_ref[me] - one_mean - centred * two_mean)
    half_ref[...] = own_ng[...].astype(BF16).reshape(cols, rows, chans)
    fcopies = send_edges(half_ref, pack, west2, east2, tops2, f_sems, lon, tiles)

    acopies = []
    for copies, own, recv, held, size, sems in (
        (ocopies, gof, gro, ago, ro, ao_sems),
        (icopies, gif, gri, agi, ri, ai_sems),
    ):
        for copy in copies:
            copy.wait()
        total = own[pl.ds(pl.multiple_of(lon * size, size), size)]
        for d in range(1, tiles):
            total = total + recv[d].astype(F32)
        held[lon] = (total * factor).astype(BF16)
        for d in range(1, tiles):
            acopies.append(push(held.at[lon], held.at[lon], sems, d, "lon", spans[d]))

    sums_ref[...] = jnp.zeros_like(sums_ref)
    extra_ref[...] = jnp.zeros_like(extra_ref)

    def tap_grad(i, _):
        mg = own_ng[pl.ds(pl.multiple_of(i * rows, rows), rows)]
        for a in range(7):
            for b in range(7):
                prod = shifts_ref[b, i + a] * mg
                sums_ref[a * 7 + b] += jnp.sum(prod.reshape(rows // 8, 8, chans), axis=0)
        return 0

    lax.fori_loop(0, cols, tap_grad, 0)
    for t in range(49):
        extra_ref[pl.ds(t, 1)] = jnp.sum(sums_ref[t], axis=0, keepdims=True)
    kcopies = [
        push(extra_ref, extras_ref.at[lon], k_sems, d, "lon", spans[d])
        for d in range(1, tiles)
    ]
    extras_ref[lon] = extra_ref[...]

    for q in range(cols):
        ext_ref[q + 3, pl.ds(8, rows)] = own_ng[pl.ds(q * rows, rows)]
    for q in range(cols + 6):
        ext_ref[q, pl.ds(8 + rows, 8)] = jnp.zeros((8, chans), F32)
    for copy in fcopies:
        copy.wait()
    for q in range(3):
        ext_ref[q, pl.ds(8, rows)] = west2[q].astype(F32)
        ext_ref[cols + 3 + q, pl.ds(8, rows)] = east2[q].astype(F32)
    for step in (-1, 0, 1):
        tile = lax.rem(partner_ref[lon] + step + tiles, tiles)
        top = tops2[tile].astype(F32)
        for q in range(cols + 6):
            if (q - 3) // cols == step:
                base = (q - 3) % cols * 3
                for s in range(3):
                    fold_ref[s, q, pl.ds(5 + s, 3 - s)] = top[base : base + 3 - s]
    fill_shifts(ext_ref, shifts_ref, rows)

    def spread(i, _):
        acc = jnp.zeros((rows, chans), F32)
        for a in range(7):
            for b in range(7):
                acc = acc + tap_ref[pl.ds(a * 7 + b, 1)] * shifts_ref[6 - b, i + 6 - a]
        fg_ref[i] = acc
        north = jnp.zeros((8, chans), F32)
        for a in range(7):
            for s in range(3):
                north = north + tap_ref[pl.ds(a * 7 + 6 - s, 1)] * fold_ref[
                    s, cols - 1 - i + 6 - a
                ]
        fg_ref[i, pl.ds(rows - 8, 8)] += north
        return 0

    lax.fori_loop(0, cols, spread, 0)

    for copy in bcopies:
        copy.wait()
    total = branch_ref[...]
    for d in range(1, n):
        total = total + brecv[d].astype(F32)
    branch_ref[...] = total
    for copy in kcopies:
        copy.wait()
    kernel_ref[...] = jnp.sum(extras_ref[...], axis=0)
    for copy in acopies:
        copy.wait()


def mega(partner, x, sg, taps, win, wout, gain, shift, factor):
    cols, rows, chans = x.shape
    cells = cols * rows
    n, _, hid = win.shape
    tiles = lax.axis_size("lon")
    width = n * chans
    ro, ri = n * hid // tiles, width // tiles
    top_rows = -(-cols * 3 // 16) * 16
    S = pltpu.VMEM
    scratch = [
        S((cols + 6, rows + 16, chans), F32), S((7, cols + 6, rows, chans), F32),
        S((3, cols + 6, 8, chans), F32), S((top_rows, chans), F32),
        S((3, rows, chans), BF16), S((3, rows, chans), BF16), S((tiles, top_rows, chans), BF16),
        S((3, rows, chans), BF16), S((3, rows, chans), BF16), S((tiles, top_rows, chans), BF16),
        S((cols, rows, chans), BF16), S((49, 8, chans), F32),
        S((tiles, 56, chans), F32), S((56, chans), F32),
        S((n, hid, chans), BF16), S((cells, chans), F32), S((n, cells, chans), BF16),
        S((n, cells, chans), BF16), S((n, cells, chans), BF16),
        S((cells, hid), BF16), S((cells, hid), F32), S((cells, hid), BF16),
        S((cells, 1), F32), S((cells, 1), F32), S((cells, chans), F32),
        S((cells, chans), F32), S((cells, chans), F32),
        S((n, cells, chans), BF16), S((n, cells, chans), BF16),
        S((n, cells, chans), BF16), S((n, cells, chans), BF16),
        S((8, cells), F32), S((n, 8, cells), F32),
        S((n * hid, chans), F32), S((width, hid), F32),
        S((width, hid), BF16), S((tiles, ri, hid), BF16),
        S((n * hid, chans), BF16), S((tiles, ro, chans), BF16),
    ]
    for count in (n,) * 5 + (tiles,) * 5 + (tiles + 1,) * 2:
        scratch += [pltpu.SemaphoreType.DMA((count,)), pltpu.SemaphoreType.DMA((count,))]
    return pl.pallas_call(
        functools.partial(mega_kernel, n, tiles, factor, 256),
        out_shape=[
            jax.ShapeDtypeStruct((cells, chans), F32),
            jax.ShapeDtypeStruct((cols, rows, chans), F32),
            jax.ShapeDtypeStruct((56, chans), F32),
            jax.ShapeDtypeStruct((tiles, ri, hid), BF16),
            jax.ShapeDtypeStruct((tiles, ro, chans), BF16),
        ],
        in_specs=[SMEM_SPEC] + [VMEM_SPEC] * 7,
        out_specs=[VMEM_SPEC] * 5,
        scratch_shapes=scratch,
        compiler_params=pltpu.CompilerParams(
            collective_id=1, has_side_effects=True, vmem_limit_bytes=LIMIT
        ),
    )(partner, x, sg, taps, win, wout, gain, shift)


def body(
    field_in, sea_mask, fold_partner, kernel, ln_gain, ln_shift, w_in, w_out, layer_scale, grad_out
):
    chans, cols, rows = field_in.shape
    tiles = lax.axis_size("lon")
    n = lax.axis_size("ch")
    cells = cols * rows
    hid = w_in.shape[1]
    factor = 1.0 / math.sqrt(tiles * cells)

    ocean_f = sea_mask.astype(F32)[None]
    masked = (field_in * sea_mask.astype(BF16)[None]).transpose(1, 2, 0)
    grad_f = grad_out.astype(F32)
    scaled_grad = (
        (ocean_f * layer_scale[:, None, None] * grad_f)
        .astype(BF16)
        .transpose(1, 2, 0)
        .reshape(cells, chans)
    )
    taps = jnp.pad(kernel.reshape(chans, 49).T, ((0, 7), (0, 0)))
    branch, field_grad, kernel_total, gw_in, gw_out = mega(
        fold_partner,
        masked,
        scaled_grad,
        taps,
        w_in.reshape(n, chans, hid),
        w_out,
        ln_gain.reshape(n, 1, chans),
        ln_shift.reshape(n, 1, chans),
        factor,
    )
    block_out = (
        ocean_f
        * (
            field_in.astype(F32)
            + layer_scale[:, None, None] * branch.T.reshape(chans, cols, rows)
        )
    ).astype(BF16)
    grad_x = (ocean_f * (grad_f + field_grad.transpose(2, 0, 1))).astype(BF16)
    kernel_grad = kernel_total[:49].T.reshape(chans, 7, 7) * factor
    gw_in = gw_in.reshape(n * chans, hid).astype(F32)
    gw_out = gw_out.reshape(n, hid, chans).transpose(1, 0, 2).reshape(hid, n * chans).astype(F32)
    return (block_out, grad_x, kernel_grad, gw_in, gw_out)


def solution(mesh):
    placed = (
        P("ch", ("grp", "lon"), None),
        P("lon", None),
        P(),
        P("ch", None, None),
        P(),
        P(),
        P(None, "ch"),
        P("ch", None),
        P("ch"),
        P("ch", ("grp", "lon"), None),
    )
    return jax.shard_map(
        body,
        mesh=mesh,
        in_specs=placed,
        out_specs=(
            P("ch", ("grp", "lon"), None),
            P("ch", ("grp", "lon"), None),
            P(("grp", "ch"), None, None),
            P("grp", "ch"),
            P(("grp", "ch"), None),
        ),
        check_vma=False,
    )
```

time: 109 us -> 80.1 us (0.73)
  between operations: 14.2 us -> 0.71 us
  Pallas kernels: 80.8 us -> 69.2 us
  local copies, waits for them, and re-layouts: 10.9 us -> 8.36 us
    pallas_call x6 -> x1, Pallas kernels: 80.8 us -> 69.2 us  [mega(): pl.pallas_call(functools.partial(mega_kernel, n, tiles, factor, 256), out...]
    unnamed x29 -> x21, local copies, waits for them, and re-layouts: 10.1 us -> 6.79 us
  transfers between devices with their start and end apart: 1 -> 0, of which waited for: 1 -> 0; matrix products, arithmetic and copies ran while one was open for 1% -> 0% of each run, Pallas kernels for 14% -> 0%
where the time goes in v2:
time: 80.1 us; the launch traced here: 79.8 us
  Pallas kernels  69.2 us (86%)
  local copies, waits for them, and re-layouts  8.36 us (10%)
  other arithmetic  1.53 us (2%)
    pallas_call x1, Pallas kernels, mega(): pl.pallas_call(functools.partial(mega_kernel, n, tiles, factor, 256), out...  69.2 us
    unnamed x21, local copies, waits for them, and re-layouts  6.79 us

profile of v2, /device:TPU:0, one launch (start us, length us, event | category | flops | bytes accessed | tf_op | source)
XLA Modules:
  0.0 79.8 jit_solution(6476575753060949592)
XLA Ops:
  0.6 0.0 copy-start.6
  0.6 0.7 copy-done.6
  1.3 0.8 reshape.41
  2.1 1.1 %copy.20 = bf16[128,8,128]{0,2,1:T(8,128)(2,1)S(1)} copy(bf16[128,8,128]{2,1,0:T(8,128)(2,1)} %param.10) | data formatting | bytes 524288 | tf_op args[0]
  3.2 0.0 copy-start.5
  3.2 0.2 multiply_bitcast_fusion.x_ref
  3.5 0.7 copy-done.5
  4.2 0.0 copy-start.7
  4.2 0.2 copy.22
  4.4 0.4 copy-done.7
  4.8 0.0 copy-start
  4.8 0.0 copy-start.1
  4.8 0.0 copy-start.2
  4.8 0.0 copy-start.3
  4.9 0.2 fusion
  5.1 0.0 copy-start.4
  5.1 0.7 copy-done
  5.8 0.1 copy-done.1
  5.9 0.0 copy-done.2
  5.9 0.0 copy-done.3
  5.9 0.0 copy-done.4
  5.9 69.2 %shard_map.137 = (f32[1024,128]{1,0:T(8,128)S(1)}, f32[8,128,128]{2,1,0:T(8,128)S(1)}, f32[56,128]{1,0:T(8,128)S(1)}, bf16[4,128,256]{2,1,0:T(8,128)(2,1)S(1)}, bf16[4,256,128]{2,1,0:T(8,128)(2,1)S(1)}) custom-call(s32[4]{0:T(128)S(1)} %copy-done.4, bf16[8,128,128]{2,1,0:T(8,128)(2,1)S(1)} %multiply_bitcast_fusion.x_ref, bf16[1024,128]{1,0:T(8,128)(2,1)S(1)} %bitcast.26, ...), custom_call_target="tpu_custom_call" | custom-call | tf_op jit(solution)/shard_map/pallas_call | solution.py:377
  75.0 0.2 fusion.2
  75.3 0.9 %copy.25 = bf16[128,8,128]{2,1,0:T(8,128)(2,1)} copy(bf16[128,8,128]{0,2,1:T(8,128)(2,1)S(1)} %get-tuple-element.25) | data formatting | bytes 524288
  76.2 0.6 mul.66
  76.8 0.9 %copy.24 = bf16[128,8,128]{2,1,0:T(8,128)(2,1)} copy(bf16[128,8,128]{0,2,1:T(8,128)(2,1)S(1)} %get-tuple-element.26) | data formatting | bytes 524288
  77.7 0.8 %bitcast_convert_fusion = f32[512,256]{1,0:T(8,128)} fusion(bf16[4,128,256]{2,1,0:T(8,128)(2,1)S(1)} %get-tuple-element.13), kind=kLoop, calls=%fused_computation.7 | loop fusion | flops 131072 | bytes 786432 | tf_op jit(solution)/shard_map/convert_element_type | solution.py:435
  78.6 0.2 copy.23
  78.8 1.0 %copy.26 = f32[256,512]{1,0:T(8,128)} copy(f32[256,512]{0,1:T(8,128)S(1)} %bitcast.31) | data formatting | bytes 1048576
  (4 shorter events, 0.1 us)
Async XLA Ops:
  0.6 0.7 copy-start.6
  3.2 1.0 %copy-start.5 = (bf16[128,8,128]{2,1,0:T(8,128)(2,1)S(1)}, bf16[128,8,128]{2,1,0:T(8,128)(2,1)}, u32[]{:S(2)}) copy-start(bf16[128,8,128]{2,1,0:T(8,128)(2,1)} %param.19) | copy-start | bytes 786436
  4.2 0.7 copy-start.7
  4.8 0.9 %copy-start = (bf16[512,256]{1,0:T(8,128)(2,1)S(1)}, bf16[512,256]{1,0:T(8,128)(2,1)}, u32[]{:S(2)}) copy-start(bf16[512,256]{1,0:T(8,128)(2,1)} %param.16) | copy-start | bytes 786436
  4.8 1.0 %copy-start.1 = (bf16[256,512]{1,0:T(8,128)(2,1)S(1)}, bf16[256,512]{1,0:T(8,128)(2,1)}, u32[]{:S(2)}) copy-start(bf16[256,512]{1,0:T(8,128)(2,1)} %wout_all.1) | copy-start | bytes 786436
  4.8 1.0 %copy-start.2 = (f32[512]{0:T(512)S(1)}, f32[512]{0:T(512)}, u32[]{:S(2)}) copy-start(f32[512]{0:T(512)} %param.14) | copy-start | bytes 6148
  4.8 1.0 %copy-start.3 = (f32[512]{0:T(512)S(1)}, f32[512]{0:T(512)}, u32[]{:S(2)}) copy-start(f32[512]{0:T(512)} %param.15) | copy-start | bytes 6148
  5.1 0.8 %copy-start.4 = (s32[4]{0:T(128)S(1)}, s32[4]{0:T(128)}, u32[]{:S(2)}) copy-start(s32[4]{0:T(128)} %partner_ref.1) | copy-start | bytes 52

commit v3 on v2

--- a/solution.py
+++ b/solution.py
@@ -100,7 +100,12 @@
     me = lax.axis_index("ch")
     lon = lax.axis_index("lon")
     greet(("ch", "lon"))
-    peers = [lax.rem(me + d, n) for d in range(n)]
+    chips = n // 2
+    chip, core = me // 2, lax.rem(me, 2)
+    peers = [
+        lax.rem(chip + d // 2, chips) * 2 + lax.rem(core + d % 2, 2) for d in range(n)
+    ]
+    far_first = list(range(2, n)) + [1]
     spans = [lax.rem(lon + d, tiles) for d in range(tiles)]
 
     def loop(step):
@@ -145,10 +150,16 @@
         mixg[me, cut] = acc.astype(BF16)
         return 0
 
-    lax.fori_loop(0, cols, conv, 0)
-    mcopies = [
-        push(mixg.at[me], mixg.at[me], m_sems, d, "ch", peers[d]) for d in range(1, n)
-    ]
+    def push_block(owner, k, slot, target):
+        view = mixg.at[owner, pl.ds(k * block, block)]
+        return push(view, view, m_sems, slot * blocks + k, "ch", target)
+
+    near, far = [], []
+    per = cols // blocks
+    for k in range(blocks):
+        lax.fori_loop(k * per, (k + 1) * per, conv, 0)
+        far.append([push_block(me, k, c, peers[2 * c]) for c in range(1, chips)])
+        near.append([push_block(me, k, 0, peers[1])])
     for copy in scopies:
         copy.wait()
 
@@ -159,8 +170,6 @@
         agrad[cut] = total
 
     loop(grads)
-    for copy in mcopies:
-        copy.wait()
 
     def forward(cut):
         parts = [mixg[j, cut].astype(F32) for j in range(n)]
@@ -183,7 +192,14 @@
         one_acc[cut] = jnp.zeros((block, chans), F32)
         two_acc[cut] = jnp.zeros((block, chans), F32)
 
-    loop(forward)
+    for k in range(blocks):
+        for c in range(1, chips):
+            far[k][c - 1].wait()
+            owner = lax.rem(chip - c + chips, chips) * 2 + core
+            near[k].append(push_block(owner, k, chips - 1 + c, peers[1]))
+        for copy in near[k]:
+            copy.wait()
+        forward(pl.ds(k * block, block))
 
     ro, ri = n * hid // tiles, width // tiles
     for j in range(n):
@@ -196,7 +212,7 @@
         ocopies.append(push(src, gro.at[d], o_sems, d, "lon", spans[d]))
 
     ncopies = []
-    for d in list(range(1, n)) + [0]:
+    for d in far_first + [0]:
         t = peers[d]
 
         def back(cut, d=d, t=t):
@@ -231,7 +247,7 @@
         icopies.append(push(src, gri.at[d], i_sems, d, "lon", spans[d]))
 
     bcopies = []
-    for d in range(1, n):
+    for d in far_first:
         t = peers[d]
 
         def out(cut, d=d, t=t):
@@ -372,7 +388,7 @@
         S((width, hid), BF16), S((tiles, ri, hid), BF16),
         S((n * hid, chans), BF16), S((tiles, ro, chans), BF16),
     ]
-    for count in (n,) * 5 + (tiles,) * 5 + (tiles + 1,) * 2:
+    for count in (cells // 256 * (n - 1),) + (n,) * 4 + (tiles,) * 5 + (tiles + 1,) * 2:
         scratch += [pltpu.SemaphoreType.DMA((count,)), pltpu.SemaphoreType.DMA((count,))]
     return pl.pallas_call(
         functools.partial(mega_kernel, n, tiles, factor, 256),

time: 80.1 us -> 76 us (0.949)
  Pallas kernels: 69.2 us -> 65.1 us
    pallas_call x1, Pallas kernels: 69.2 us -> 65.1 us  [mega(): pl.pallas_call(functools.partial(mega_kernel, n, tiles, factor, 256), out...]
where the time goes in v3:
time: 76 us; the launch traced here: 75.7 us
  Pallas kernels  65.1 us (86%)
  local copies, waits for them, and re-layouts  8.36 us (11%)
  other arithmetic  1.53 us (2%)
    pallas_call x1, Pallas kernels, mega(): pl.pallas_call(functools.partial(mega_kernel, n, tiles, factor, 256), out...  65.1 us
    unnamed x21, local copies, waits for them, and re-layouts  6.79 us

profile of v3, /device:TPU:0, one launch (start us, length us, event | category | flops | bytes accessed | tf_op | source)
XLA Modules:
  0.0 75.7 jit_solution(16534669243105596933)
XLA Ops:
  0.6 0.0 copy-start.6
  0.6 0.7 copy-done.6
  1.3 0.8 reshape.41
  2.1 1.1 %copy.20 = bf16[128,8,128]{0,2,1:T(8,128)(2,1)S(1)} copy(bf16[128,8,128]{2,1,0:T(8,128)(2,1)} %param.10) | data formatting | bytes 524288 | tf_op args[0]
  3.2 0.0 copy-start.5
  3.2 0.2 multiply_bitcast_fusion.x_ref
  3.5 0.7 copy-done.5
  4.2 0.0 copy-start.7
  4.2 0.2 copy.22
  4.4 0.4 copy-done.7
  4.8 0.0 copy-start
  4.8 0.0 copy-start.1
  4.8 0.0 copy-start.2
  4.8 0.0 copy-start.3
  4.9 0.2 fusion
  5.1 0.0 copy-start.4
  5.1 0.7 copy-done
  5.8 0.1 copy-done.1
  5.9 0.0 copy-done.2
  5.9 0.0 copy-done.3
  5.9 0.0 copy-done.4
  5.9 65.1 %shard_map.137 = (f32[1024,128]{1,0:T(8,128)S(1)}, f32[8,128,128]{2,1,0:T(8,128)S(1)}, f32[56,128]{1,0:T(8,128)S(1)}, bf16[4,128,256]{2,1,0:T(8,128)(2,1)S(1)}, bf16[4,256,128]{2,1,0:T(8,128)(2,1)S(1)}) custom-call(s32[4]{0:T(128)S(1)} %copy-done.4, bf16[8,128,128]{2,1,0:T(8,128)(2,1)S(1)} %multiply_bitcast_fusion.x_ref, bf16[1024,128]{1,0:T(8,128)(2,1)S(1)} %bitcast.26, ...), custom_call_target="tpu_custom_call" | custom-call | tf_op jit(solution)/shard_map/pallas_call | solution.py:393
  71.0 0.2 fusion.2
  71.2 0.9 %copy.25 = bf16[128,8,128]{2,1,0:T(8,128)(2,1)} copy(bf16[128,8,128]{0,2,1:T(8,128)(2,1)S(1)} %get-tuple-element.25) | data formatting | bytes 524288
  72.1 0.6 mul.66
  72.7 0.9 %copy.24 = bf16[128,8,128]{2,1,0:T(8,128)(2,1)} copy(bf16[128,8,128]{0,2,1:T(8,128)(2,1)S(1)} %get-tuple-element.26) | data formatting | bytes 524288
  73.6 0.8 %bitcast_convert_fusion = f32[512,256]{1,0:T(8,128)} fusion(bf16[4,128,256]{2,1,0:T(8,128)(2,1)S(1)} %get-tuple-element.13), kind=kLoop, calls=%fused_computation.7 | loop fusion | flops 131072 | bytes 786432 | tf_op jit(solution)/shard_map/convert_element_type | solution.py:451
  74.5 0.2 copy.23
  74.7 1.0 %copy.26 = f32[256,512]{1,0:T(8,128)} copy(f32[256,512]{0,1:T(8,128)S(1)} %bitcast.31) | data formatting | bytes 1048576
  (4 shorter events, 0.1 us)
Async XLA Ops:
  0.6 0.7 copy-start.6
  3.2 1.0 %copy-start.5 = (bf16[128,8,128]{2,1,0:T(8,128)(2,1)S(1)}, bf16[128,8,128]{2,1,0:T(8,128)(2,1)}, u32[]{:S(2)}) copy-start(bf16[128,8,128]{2,1,0:T(8,128)(2,1)} %param.19) | copy-start | bytes 786436
  4.2 0.7 copy-start.7
  4.8 0.9 %copy-start = (bf16[512,256]{1,0:T(8,128)(2,1)S(1)}, bf16[512,256]{1,0:T(8,128)(2,1)}, u32[]{:S(2)}) copy-start(bf16[512,256]{1,0:T(8,128)(2,1)} %param.16) | copy-start | bytes 786436
  4.8 1.0 %copy-start.1 = (bf16[256,512]{1,0:T(8,128)(2,1)S(1)}, bf16[256,512]{1,0:T(8,128)(2,1)}, u32[]{:S(2)}) copy-start(bf16[256,512]{1,0:T(8,128)(2,1)} %wout_all.1) | copy-start | bytes 786436
  4.8 1.0 %copy-start.2 = (f32[512]{0:T(512)S(1)}, f32[512]{0:T(512)}, u32[]{:S(2)}) copy-start(f32[512]{0:T(512)} %param.14) | copy-start | bytes 6148
  4.8 1.0 %copy-start.3 = (f32[512]{0:T(512)S(1)}, f32[512]{0:T(512)}, u32[]{:S(2)}) copy-start(f32[512]{0:T(512)} %param.15) | copy-start | bytes 6148
  5.1 0.8 %copy-start.4 = (s32[4]{0:T(128)S(1)}, s32[4]{0:T(128)}, u32[]{:S(2)}) copy-start(s32[4]{0:T(128)} %partner_ref.1) | copy-start | bytes 52

commit v4 on v3

--- a/solution.py
+++ b/solution.py
@@ -117,7 +117,8 @@
 
     pack[...] = jnp.zeros_like(pack)
     ecopies = send_edges(x_ref, pack, west, east, tops, e_sems, lon, tiles)
-    scopies = [push(sg_ref, sgg.at[me], s_sems, d, "ch", peers[d]) for d in range(1, n)]
+    sfar = [push(sg_ref, sgg.at[me], s_sems, c, "ch", peers[2 * c]) for c in range(1, chips)]
+    scopies = [push(sg_ref, sgg.at[me], s_sems, 0, "ch", peers[1])]
     sgg[me] = sg_ref[...]
     for j in range(n):
         wout_ref[j] = wout_all[:, j * chans : (j + 1) * chans]
@@ -127,6 +128,10 @@
         ext_ref[q + 3, pl.ds(8, rows)] = x_ref[q].astype(F32)
     for copy in ecopies:
         copy.wait()
+    for c in range(1, chips):
+        sfar[c - 1].wait()
+        view = sgg.at[lax.rem(chip - c + chips, chips) * 2 + core]
+        scopies.append(push(view, view, s_sems, chips - 1 + c, "ch", peers[1]))
 
     for q in range(3):
         ext_ref[q, pl.ds(8, rows)] = west[q].astype(F32)

time: 76 us -> 73.4 us (0.966)
  Pallas kernels: 65.1 us -> 62.5 us
    pallas_call x1, Pallas kernels: 65.1 us -> 62.5 us  [mega(): pl.pallas_call(functools.partial(mega_kernel, n, tiles, factor, 256), out...]
where the time goes in v4:
time: 73.4 us; the launch traced here: 73.1 us
  Pallas kernels  62.5 us (85%)
  local copies, waits for them, and re-layouts  8.36 us (11%)
  other arithmetic  1.53 us (2%)
    pallas_call x1, Pallas kernels, mega(): pl.pallas_call(functools.partial(mega_kernel, n, tiles, factor, 256), out...  62.5 us
    unnamed x21, local copies, waits for them, and re-layouts  6.79 us

profile of v4, /device:TPU:0, one launch (start us, length us, event | category | flops | bytes accessed | tf_op | source)
XLA Modules:
  0.0 73.1 jit_solution(16003659226804943473)
XLA Ops:
  0.6 0.0 copy-start.6
  0.6 0.7 copy-done.6
  1.3 0.8 %reshape.41 = f32[128,49]{0,1:T(8,128)S(1)} reshape(f32[128,7,7]{0,2,1:T(8,128)} %param.13) | data formatting | bytes 50176 | tf_op jit(solution)/shard_map/reshape | solution.py:435
  2.1 1.1 %copy.20 = bf16[128,8,128]{0,2,1:T(8,128)(2,1)S(1)} copy(bf16[128,8,128]{2,1,0:T(8,128)(2,1)} %param.10) | data formatting | bytes 524288 | tf_op args[0]
  3.2 0.0 copy-start.5
  3.2 0.2 multiply_bitcast_fusion.x_ref
  3.5 0.7 %copy-done.5 = bf16[128,8,128]{2,1,0:T(8,128)(2,1)S(1)} copy-done((bf16[128,8,128]{2,1,0:T(8,128)(2,1)S(1)}, bf16[128,8,128]{2,1,0:T(8,128)(2,1)}, u32[]{:S(2)}) %copy-start.5) | copy-done | bytes 262168
  4.2 0.0 copy-start.7
  4.2 0.2 copy.22
  4.4 0.4 copy-done.7
  4.8 0.0 copy-start
  4.8 0.0 copy-start.1
  4.8 0.0 copy-start.2
  4.8 0.0 copy-start.3
  4.9 0.2 fusion
  5.1 0.0 copy-start.4
  5.1 0.7 copy-done
  5.8 0.1 copy-done.1
  5.9 0.0 copy-done.2
  5.9 0.0 copy-done.3
  5.9 0.0 copy-done.4
  5.9 62.5 %shard_map.137 = (f32[1024,128]{1,0:T(8,128)S(1)}, f32[8,128,128]{2,1,0:T(8,128)S(1)}, f32[56,128]{1,0:T(8,128)S(1)}, bf16[4,128,256]{2,1,0:T(8,128)(2,1)S(1)}, bf16[4,256,128]{2,1,0:T(8,128)(2,1)S(1)}) custom-call(s32[4]{0:T(128)S(1)} %copy-done.4, bf16[8,128,128]{2,1,0:T(8,128)(2,1)S(1)} %multiply_bitcast_fusion.x_ref, bf16[1024,128]{1,0:T(8,128)(2,1)S(1)} %bitcast.26, ...), custom_call_target="tpu_custom_call" | custom-call | tf_op jit(solution)/shard_map/pallas_call | solution.py:398
  68.3 0.2 fusion.2
  68.6 0.9 %copy.25 = bf16[128,8,128]{2,1,0:T(8,128)(2,1)} copy(bf16[128,8,128]{0,2,1:T(8,128)(2,1)S(1)} %get-tuple-element.25) | data formatting | bytes 524288
  69.5 0.6 mul.66
  70.1 0.9 %copy.24 = bf16[128,8,128]{2,1,0:T(8,128)(2,1)} copy(bf16[128,8,128]{0,2,1:T(8,128)(2,1)S(1)} %get-tuple-element.26) | data formatting | bytes 524288
  71.0 0.8 %bitcast_convert_fusion = f32[512,256]{1,0:T(8,128)} fusion(bf16[4,128,256]{2,1,0:T(8,128)(2,1)S(1)} %get-tuple-element.13), kind=kLoop, calls=%fused_computation.7 | loop fusion | flops 131072 | bytes 786432 | tf_op jit(solution)/shard_map/convert_element_type | solution.py:456
  71.9 0.2 copy.23
  72.1 1.0 %copy.26 = f32[256,512]{1,0:T(8,128)} copy(f32[256,512]{0,1:T(8,128)S(1)} %bitcast.31) | data formatting | bytes 1048576
  (4 shorter events, 0.1 us)
Async XLA Ops:
  0.6 0.7 copy-start.6
  3.2 1.0 %copy-start.5 = (bf16[128,8,128]{2,1,0:T(8,128)(2,1)S(1)}, bf16[128,8,128]{2,1,0:T(8,128)(2,1)}, u32[]{:S(2)}) copy-start(bf16[128,8,128]{2,1,0:T(8,128)(2,1)} %param.19) | copy-start | bytes 786436
  4.2 0.7 copy-start.7
  4.8 0.9 %copy-start = (bf16[512,256]{1,0:T(8,128)(2,1)S(1)}, bf16[512,256]{1,0:T(8,128)(2,1)}, u32[]{:S(2)}) copy-start(bf16[512,256]{1,0:T(8,128)(2,1)} %param.16) | copy-start | bytes 786436
  4.8 1.0 %copy-start.1 = (bf16[256,512]{1,0:T(8,128)(2,1)S(1)}, bf16[256,512]{1,0:T(8,128)(2,1)}, u32[]{:S(2)}) copy-start(bf16[256,512]{1,0:T(8,128)(2,1)} %wout_all.1) | copy-start | bytes 786436
  4.8 1.0 %copy-start.2 = (f32[512]{0:T(512)S(1)}, f32[512]{0:T(512)}, u32[]{:S(2)}) copy-start(f32[512]{0:T(512)} %param.14) | copy-start | bytes 6148
  4.8 1.0 %copy-start.3 = (f32[512]{0:T(512)S(1)}, f32[512]{0:T(512)}, u32[]{:S(2)}) copy-start(f32[512]{0:T(512)} %param.15) | copy-start | bytes 6148
  5.1 0.8 %copy-start.4 = (s32[4]{0:T(128)S(1)}, s32[4]{0:T(128)}, u32[]{:S(2)}) copy-start(s32[4]{0:T(128)} %partner_ref.1) | copy-start | bytes 52
